TPU v7x, 128 devices: a whole 4x4x4 slice. The times are simulated.
128 devices in a mesh: dp: 16 (over x, y_hi, core), mp: 8 (over y_lo, z).
Axes of the slice: x: 4, y: 4 (y_hi: 2, y_lo: 2; y = y_hi * 2 + y_lo), z: 4, core: 2. Of those that a mesh axis runs over, the one named last changes fastest.
Arguments:
- tokens_in: bfloat16 [16384, 2048], P(('dp', 'mp')), may hold values from -6 to 6
- cotangent: bfloat16 [16384, 2048], P(('dp', 'mp')), may hold values from -6 to 6
- lengths: int32 [16, 3], P('dp'), may hold values from 0 to 1024, as said below
- ln1_gain: float32 [2048], replicated, may hold values from 0.5 to 1.5
- ln1_bias: float32 [2048], replicated, may hold values from -1 to 1
- w_query: bfloat16 [2048, 2048], P(None, 'mp'), may hold values from -0.125 to 0.125
- w_key: bfloat16 [2048, 2048], P(None, 'mp'), may hold values from -0.125 to 0.125
- w_value: bfloat16 [2048, 4096], P(None, 'mp'), may hold values from -0.125 to 0.125
- w_gate: bfloat16 [2048, 4096], P(None, 'mp'), may hold values from -0.125 to 0.125
- w_out: bfloat16 [4096, 2048], P('mp'), may hold values from -0.125 to 0.125
- ln2_gain: float32 [2048], replicated, may hold values from 0.5 to 1.5
- ln2_bias: float32 [2048], replicated, may hold values from -1 to 1
- w_up: bfloat16 [2048, 4096], P(None, 'mp'), may hold values from -0.125 to 0.125
- b_up: float32 [4096], P('mp'), may hold values from -1.5 to 1.5
- w_down: bfloat16 [4096, 2048], P('mp'), may hold values from -0.125 to 0.125
- b_down: float32 [2048], replicated, may hold values from -1 to 1
Outputs:
- out: bfloat16 [16384, 2048], P(('dp', 'mp'))
- grad_x: float32 [16384, 2048], P(('dp', 'mp'))
- grad_ln1_gain: float32 [2048], replicated
- grad_ln1_bias: float32 [2048], replicated
- grad_query: float32 [2048, 2048], P(None, 'mp')
- grad_key: float32 [2048, 2048], P(None, 'mp')
- grad_value: float32 [2048, 4096], P(None, 'mp')
- grad_gate: float32 [2048, 4096], P(None, 'mp')
- grad_out: float32 [4096, 2048], P('mp')
- grad_ln2_gain: float32 [2048], replicated
- grad_ln2_bias: float32 [2048], replicated
- grad_up: float32 [2048, 4096], P(None, 'mp')
- grad_b_up: float32 [4096], P('mp')
- grad_down: float32 [4096, 2048], P('mp')
- grad_b_down: float32 [2048], replicated
Inputs may be any that keep to these rules, and one draw needn't show every extreme that they name: `lengths`: each row gives, in order, three documents that fill the group's 1024 tokens: the first and the last hold fewer than 128 tokens each (possibly none), so the middle one reaches from the group's first 128 tokens into its last 128; in at least one group the middle one fills all 1024 tokens.
All inputs are finite; a program needn't handle non-finite values.
Results may differ from a plain program's by a relative error of at most 0.03.
Values may be sent and summed in bfloat16 or wider, within the bound.
No kernel may reach another device: no remote copies, remote signals or barrier semaphores. Data moves between devices by JAX's collectives and lax.ppermute only.
A program may use at most 192 MiB of HBM per device.

v0:
```python
import math

import jax
import jax.numpy as jnp
from jax import lax
from jax.sharding import Mesh
from jax.sharding import PartitionSpec as P

DK = 256
DV = 512
MP = ("mp_0", "mp_1")
DP_MP = ("dp", "mp_0", "mp_1")


norm_eps = 1e-05
group_eps = 1.0


def laid_out(pieces, dim):
    pieces = jnp.moveaxis(pieces, 0, dim)
    dims = pieces.shape
    return pieces.reshape(*dims[:dim], dims[dim] * dims[dim + 1], *dims[dim + 2 :])


def stacked_from(value, axes, order):
    pieces = value[None]
    for k in order:
        pieces = lax.all_gather(pieces, axes[k], axis=0, tiled=True)
    current = [lax.axis_size(axes[k]) for k in reversed(order)]
    pieces = pieces.reshape(*current, *value.shape)
    turned = sorted(range(len(order)), key=lambda place: order[len(order) - 1 - place])
    return pieces.transpose(*turned, *range(len(order), pieces.ndim)).reshape(-1, *value.shape)


def gathered_by_axis(value, axes, order, dim):
    return laid_out(stacked_from(value, axes, order), dim)


def cut_along(value, dim, size):
    dims = value.shape
    pieces = value.reshape(*dims[:dim], size, dims[dim] // size, *dims[dim + 1 :])
    return jnp.moveaxis(pieces, dim, 0)


def sum_at_owner(value, axis, dim):
    pieces = cut_along(value, dim, lax.axis_size(axis))
    arrived = lax.all_to_all(pieces, axis, split_axis=0, concat_axis=0, tiled=True)
    return arrived.astype(jnp.float32).sum(axis=0)


def layer_norm(inputs, gain_vec, bias_vec):
    centre = inputs - jnp.mean(inputs, -1, keepdims=True)
    spread = jnp.mean(centre * centre, -1, keepdims=True)
    return centre * lax.rsqrt(spread + norm_eps) * gain_vec + bias_vec


def rotate(inputs, cosine, sine_table):
    paired = inputs.reshape(inputs.shape[:-1] + (inputs.shape[-1] // 2, 2))
    turned = jnp.stack([-paired[..., 1], paired[..., 0]], -1).reshape(inputs.shape)
    return inputs * cosine + turned * sine_table


def layout(length_row, token_count):
    doc_ends = jnp.cumsum(length_row)
    doc_starts = doc_ends - length_row
    tokens = jnp.arange(token_count, dtype=jnp.int32)
    member = (tokens[:, None] >= doc_starts[None, :]) & (tokens[:, None] < doc_ends[None, :])
    numbers = jnp.arange(length_row.shape[0], dtype=jnp.int32)
    doc_ids = jnp.sum(jnp.where(member, numbers[None, :], 0), -1)
    offsets = jnp.sum(jnp.where(member, doc_starts[None, :], 0), -1)
    return (doc_ids, tokens - offsets)


def angles(positions, head_width):
    half_width = head_width // 2
    ladder = jnp.arange(half_width, dtype=jnp.float32) / max(half_width - 1, 1)
    frequency = jnp.repeat(jnp.exp(-math.log(10000.0) * ladder), 2)
    phases = positions.astype(jnp.float32)[:, None] * frequency[None, :]
    return (jnp.cos(phases)[:, None, :], jnp.sin(phases)[:, None, :])


def decay_mask(row_docs, row_start, doc_ids, log_decay, block_len, group_tok):
    row_index = row_start + jnp.arange(block_len, dtype=jnp.int32)
    col_index = jnp.arange(group_tok, dtype=jnp.int32)
    distance = row_index[:, None] - col_index[None, :]
    visible = (distance >= 0) & (row_docs[:, None] == doc_ids[None, :])
    span_float = jnp.maximum(distance, 0).astype(log_decay.dtype)
    return jnp.where(visible[None], jnp.exp(span_float[None] * log_decay[:, None, None]), 0.0)


def gate_norm(retained, gate_pre):
    scale_inv = lax.rsqrt(jnp.mean(retained * retained, -1, keepdims=True) + group_eps)
    return jax.nn.silu(gate_pre) * (retained * scale_inv).reshape(gate_pre.shape)


def contract_rows(left_side, right_side):
    return lax.dot_general(
        left_side, right_side, (((0,), (0,)), ((), ())), preferred_element_type=jnp.float32
    )


def contract_cols(left_side, right_side):
    return lax.dot_general(
        left_side, right_side, (((1,), (1,)), ((), ())), preferred_element_type=jnp.float32
    )


def local(
    tokens_in,
    cotangent,
    lengths,
    ln1_gain,
    ln1_bias,
    w_query,
    w_key,
    w_value,
    w_gate,
    w_out,
    ln2_gain,
    ln2_bias,
    w_up,
    b_up,
    w_down,
    b_down,
):
    tok_rows = tokens_in.shape[0]
    group_tok = tok_rows * lax.axis_size(MP)
    block_len = min(512, group_tok)
    block_count = group_tok // block_len
    heads_here = w_query.shape[1] // DK
    doc_ids, positions = layout(lengths[0], group_tok)
    cosine, sine_table = angles(positions, DK)
    head_ids = lax.axis_index(MP) * heads_here + jnp.arange(heads_here, dtype=jnp.int32)
    log_decay = jnp.log1p(-jnp.exp2(-5.0 - head_ids.astype(jnp.float32)))
    row_starts = jnp.arange(block_count, dtype=jnp.int32) * block_len
    inputs = tokens_in.astype(jnp.float32)
    normed = layer_norm(inputs, ln1_gain, ln1_bias).astype(jnp.bfloat16)
    gathered = lax.all_gather(normed, MP, axis=0, tiled=True)
    queries = jnp.dot(gathered, w_query, preferred_element_type=jnp.float32).reshape(
        group_tok, heads_here, DK
    )
    keys_all = jnp.dot(gathered, w_key, preferred_element_type=jnp.float32).reshape(
        group_tok, heads_here, DK
    )
    values = (
        jnp.dot(gathered, w_value, preferred_element_type=jnp.float32)
        .astype(jnp.bfloat16)
        .reshape(group_tok, heads_here, DV)
    )
    gate_pre = jnp.dot(gathered, w_gate, preferred_element_type=jnp.float32)
    query_rot = rotate(queries, cosine, sine_table).astype(jnp.bfloat16)
    key_rot = rotate(keys_all, cosine, sine_table).astype(jnp.bfloat16)
    query_blocks = query_rot.reshape(block_count, block_len, heads_here, DK)

    def block_scores(query_rows, row_start):
        row_docs = lax.dynamic_slice_in_dim(doc_ids, row_start, block_len, 0)
        weights_mask = decay_mask(row_docs, row_start, doc_ids, log_decay, block_len, group_tok)
        raw_scores = jnp.einsum(
            "qhd,khd->hqk", query_rows, key_rot, preferred_element_type=jnp.float32
        )
        return (weights_mask, (raw_scores * weights_mask).astype(jnp.bfloat16))

    def retain(members):
        scores = block_scores(members[0], members[1])[1]
        return jnp.einsum("hqk,khe->qhe", scores, values, preferred_element_type=jnp.float32)

    retained = lax.map(retain, (query_blocks, row_starts)).reshape(group_tok, heads_here, DV)
    gated = gate_norm(retained, gate_pre).astype(jnp.bfloat16)
    middle = inputs + lax.psum_scatter(
        jnp.dot(gated, w_out, preferred_element_type=jnp.float32),
        MP,
        scatter_dimension=0,
        tiled=True,
    )
    normed_two = layer_norm(middle, ln2_gain, ln2_bias).astype(jnp.bfloat16)
    gathered_two = gathered_by_axis(normed_two, MP, (0, 1), 0)
    pre_act = jnp.dot(gathered_two, w_up, preferred_element_type=jnp.float32) + b_up
    hidden = jax.nn.gelu(pre_act, approximate=False).astype(jnp.bfloat16)
    result = (
        middle
        + lax.psum_scatter(
            jnp.dot(hidden, w_down, preferred_element_type=jnp.float32).astype(jnp.bfloat16),
            MP,
            scatter_dimension=0,
            tiled=True,
        ).astype(jnp.float32)
        + b_down
    )
    grad_y = cotangent.astype(jnp.float32)
    grad_b_down = jnp.sum(grad_y, 0)
    cot_all = lax.all_gather(cotangent, MP, axis=0, tiled=True)
    grad_down_w = contract_rows(hidden, cot_all)
    grad_hidden = contract_cols(cot_all, w_down)
    _, gelu_pull = jax.vjp(lambda inner: jax.nn.gelu(inner, approximate=False), pre_act)
    grad_pre = gelu_pull(grad_hidden)[0].astype(jnp.bfloat16)
    grad_up_w = contract_rows(gathered_two, grad_pre)
    grad_b_up = jnp.sum(grad_pre, 0, dtype=jnp.float32)
    grad_normed_two = lax.psum_scatter(
        contract_cols(grad_pre, w_up), MP, scatter_dimension=0, tiled=True
    )
    _, second_pull = jax.vjp(layer_norm, middle, ln2_gain, ln2_bias)
    grad_mid_part, grad_ln2_gain, grad_ln2_bias = second_pull(grad_normed_two)
    grad_middle = grad_y + grad_mid_part
    branch_all = lax.all_gather(grad_middle.astype(jnp.bfloat16), MP, axis=0, tiled=True)
    grad_out_w = contract_rows(gated, branch_all)
    grad_gated = contract_cols(branch_all, w_out)
    _, gate_pull = jax.vjp(gate_norm, retained, gate_pre)
    grad_retained, grad_gate_pre = gate_pull(grad_gated)
    grad_ret_low = grad_retained.astype(jnp.bfloat16)
    grad_gate_low = grad_gate_pre.astype(jnp.bfloat16)
    grad_blocks = grad_ret_low.reshape(block_count, block_len, heads_here, DV)

    def retain_back(carried, members):
        key_acc, value_acc = carried
        query_rows, grad_rows, row_start = members
        weights_mask, scores = block_scores(query_rows, row_start)
        grad_scores = jnp.einsum(
            "qhe,khe->hqk", grad_rows, values, preferred_element_type=jnp.float32
        )
        grad_raw = (grad_scores * weights_mask).astype(jnp.bfloat16)
        grad_query_rows = jnp.einsum(
            "hqk,khd->qhd", grad_raw, key_rot, preferred_element_type=jnp.float32
        )
        key_acc = key_acc + jnp.einsum(
            "hqk,qhd->khd", grad_raw, query_rows, preferred_element_type=jnp.float32
        )
        value_acc = value_acc + jnp.einsum(
            "hqk,qhe->khe", scores, grad_rows, preferred_element_type=jnp.float32
        )
        return ((key_acc, value_acc), grad_query_rows)

    start_acc = (
        jnp.zeros((group_tok, heads_here, DK), jnp.float32),
        jnp.zeros((group_tok, heads_here, DV), jnp.float32),
    )
    (grad_key_rot, grad_values), grad_query_rot = lax.scan(
        retain_back, start_acc, (query_blocks, grad_blocks, row_starts)
    )
    grad_query_rot = grad_query_rot.reshape(group_tok, heads_here, DK)
    _, rotate_pull = jax.vjp(lambda inner: rotate(inner, cosine, sine_table), queries)
    grad_query_low = (
        rotate_pull(grad_query_rot)[0].astype(jnp.bfloat16).reshape(group_tok, heads_here * DK)
    )
    grad_key_low = (
        rotate_pull(grad_key_rot)[0].astype(jnp.bfloat16).reshape(group_tok, heads_here * DK)
    )
    grad_value_low = grad_values.astype(jnp.bfloat16).reshape(group_tok, heads_here * DV)
    grad_query_w = contract_rows(gathered, grad_query_low)
    grad_key_w = contract_rows(gathered, grad_key_low)
    grad_value_w = contract_rows(gathered, grad_value_low)
    grad_gate_w = contract_rows(gathered, grad_gate_low)
    total_sum = contract_cols(grad_query_low, w_query) + contract_cols(grad_key_low, w_key)
    grad_normed = sum_at_owner(
        (
            total_sum
            + contract_cols(grad_value_low, w_value)
            + contract_cols(grad_gate_low, w_gate)
        ).astype(jnp.bfloat16),
        MP,
        0,
    )
    _, first_pull = jax.vjp(layer_norm, inputs, ln1_gain, ln1_bias)
    grad_in_part, grad_ln1_gain, grad_ln1_bias = first_pull(grad_normed)
    grad_x = grad_middle + grad_in_part
    norm_sums = lax.psum(
        (grad_ln1_gain, grad_ln1_bias, grad_ln2_gain, grad_ln2_bias, grad_b_down), DP_MP
    )
    weight_sums = (
        lax.psum(grad_query_w.astype(jnp.bfloat16), "dp").astype(jnp.float32),
        lax.psum(grad_key_w.astype(jnp.bfloat16), "dp").astype(jnp.float32),
        lax.psum(grad_value_w.astype(jnp.bfloat16), "dp").astype(jnp.float32),
        lax.psum(grad_gate_w.astype(jnp.bfloat16), "dp").astype(jnp.float32),
        lax.psum(grad_out_w.astype(jnp.bfloat16), "dp").astype(jnp.float32),
        lax.psum(grad_up_w.astype(jnp.bfloat16), "dp").astype(jnp.float32),
        lax.psum(grad_b_up.astype(jnp.bfloat16), "dp").astype(jnp.float32),
        lax.psum(grad_down_w.astype(jnp.bfloat16), "dp").astype(jnp.float32),
    )
    return (
        result.astype(jnp.bfloat16),
        grad_x,
        norm_sums[0],
        norm_sums[1],
        weight_sums[0],
        weight_sums[1],
        weight_sums[2],
        weight_sums[3],
        weight_sums[4],
        norm_sums[2],
        norm_sums[3],
        weight_sums[5],
        weight_sums[6],
        weight_sums[7],
        norm_sums[4],
    )


def solution(mesh):
    split = Mesh(mesh.devices.reshape(mesh.shape["dp"], 2, 4), ("dp", "mp_0", "mp_1"))
    return jax.shard_map(
        local,
        mesh=split,
        in_specs=(
            P(DP_MP, None),
            P(DP_MP, None),
            P("dp", None),
            P(),
            P(),
            P(None, MP),
            P(None, MP),
            P(None, MP),
            P(None, MP),
            P(MP, None),
            P(),
            P(),
            P(None, MP),
            P(MP),
            P(MP, None),
            P(),
        ),
        out_specs=(
            P(DP_MP, None),
            P(DP_MP, None),
            P(),
            P(),
            P(None, MP),
            P(None, MP),
            P(None, MP),
            P(None, MP),
            P(MP, None),
            P(),
            P(),
            P(None, MP),
            P(MP),
            P(MP, None),
            P(),
        ),
        check_vma=False,
    )
```

profile of v0, /device:TPU:0, one launch (start us, length us, event | category | flops | bytes accessed | tf_op | source)
XLA Modules:
  0.0 1042.4 jit_solution(3534256559234635536)
XLA Ops:
  14.0 54.7 %all-gather.7.cloned.1.call-done = bf16[1024,2048]{1,0:T(8,128)(2,1)} async-done(((bf16[128,2048]{1,0:T(8,128)(2,1)}), bf16[1024,2048]{1,0:T(8,128)(2,1)}) %all-gather.7.cloned.1.call-update) | async-done | bytes 4194320 | tf_op jit(solution)/shard_map/all_gather | solution.py:138
  99.2 6.1 fusion.86
  110.7 13.9 %while.25 = (s32[]{:T(128)}, f32[2,512,1,512]{3,1,2,0:T(8,128)}, bf16[2,512,1,256]{3,1,2,0:T(8,128)(2,1)S(1)}, bf16[1024,1,256]{2,0,1:T(8,128)(2,1)S(1)}, s32[2]...) while((s32[]{:T(128)}, f32[2,512,1,512]{3,1,2,0:T(8,128)}, ...), condition=%wide.region_6.7_spmd, body=%wide.region_5.6_spmd.sunk | while | flops 810549760 | bytes 2899627 | solution.py:167
  127.3 6.9 multiply_convert_fusion.4
  135.2 5.6 fusion.102
  140.9 91.6 %reduce-scatter.4.cloned.1.call-done = f32[128,2048]{1,0:T(8,128)} async-done(((f32[1024,2048]{1,0:T(8,128)}), f32[128,2048]{1,0:T(8,128)}) %reduce-scatter.4.cloned.1.call-update) | async-done | bytes 1048592 | tf_op jit(solution)/shard_map/reduce_scatter | solution.py:169
  235.4 22.6 %all-gather.15.cloned.1.call-done = bf16[256,2048]{1,0:T(8,128)(2,1)} async-done(((bf16[128,2048]{1,0:T(8,128)(2,1)}), bf16[256,2048]{1,0:T(8,128)(2,1)}) %all-gather.15.cloned.1.call-update) | async-done | bytes 1048592 | tf_op jit(solution)/shard_map/all_gather | solution.py:28
  258.6 50.4 %all-gather.9.cloned.1.call-done = bf16[8,128,2048]{2,1,0:T(8,128)(2,1)} async-done(((bf16[2,128,2048]{2,1,0:T(8,128)(2,1)}), bf16[8,128,2048]{2,1,0:T(8,128)(2,1)}) %all-gather.9.cloned.1.call-update) | async-done | bytes 4194320 | tf_op jit(solution)/shard_map/all_gather | solution.py:28
  317.3 46.2 %all-gather.11.cloned.1.call-done = bf16[1024,2048]{1,0:T(8,128)(2,1)} async-done(((bf16[128,2048]{1,0:T(8,128)(2,1)}), bf16[1024,2048]{1,0:T(8,128)(2,1)}) %all-gather.11.cloned.1.call-update) | async-done | bytes 4194320 | tf_op jit(solution)/shard_map/all_gather | solution.py:191
  363.5 21.0 %fusion.94 = (bf16[512]{0:T(512)(128)(2,1)S(1)}, bf16[1024,512]{1,0:T(8,128)(2,1)S(1)}, f32[1024,512]{1,0:T(8,128)}) fusion(f32[1024,512]{1,0:T(8,128)} %fusion.103, f32[512]{0:T(512)S(1)} %copy-done.41, bf16[1024,2048]{1,0:T(8,128)(2,1)} %all-gather.11.cloned.1.call-done, bf16[512,2048]{1,0:T(8,128)(2,1)S(1)} %copy-done), kind=kOutput, calls=%fused_computation.173 | convolution fusion | flops 2186280448 | bytes 11537408 | tf_op jit(solution)/shard_map/dot_general | solution.py:103
  385.5 5.6 fusion.104
  399.6 83.3 %reduce-scatter.8.cloned.1.call-done = f32[128,2048]{1,0:T(8,128)} async-done(((f32[1024,2048]{1,0:T(8,128)}), f32[128,2048]{1,0:T(8,128)}) %reduce-scatter.8.cloned.1.call-update) | async-done | bytes 1048592 | tf_op jit(solution)/shard_map/reduce_scatter | solution.py:198
  484.5 53.3 %reduce-scatter.6.cloned.1.call-done = bf16[128,2048]{1,0:T(8,128)(2,1)} async-done(((bf16[1024,2048]{1,0:T(8,128)(2,1)}), bf16[128,2048]{1,0:T(8,128)(2,1)}) %reduce-scatter.6.cloned.1.call-update) | async-done | bytes 524304 | tf_op jit(solution)/shard_map/reduce_scatter | solution.py:181
  542.2 6.0 convolution_convert_fusion.2
  552.0 41.0 %all-gather.13.cloned.1.call-done = bf16[1024,2048]{1,0:T(8,128)(2,1)} async-done(((bf16[128,2048]{1,0:T(8,128)(2,1)}), bf16[1024,2048]{1,0:T(8,128)(2,1)}) %all-gather.13.cloned.1.call-update) | async-done | bytes 4194320 | tf_op jit(solution)/shard_map/all_gather | solution.py:204
  593.0 6.9 fusion.47
  603.2 24.0 %while.26 = (s32[]{:T(128)}, f32[1024,1,256]{0,2,1:T(8,128)S(1)}, f32[1024,1,512]{0,2,1:T(8,128)}, f32[2,512,1,256]{3,1,2,0:T(8,128)}, bf16[2,512,1,256]{3,1,2,0...) while((s32[]{:T(128)}, f32[1024,1,256]{0,2,1:T(8,128)S(1)}, ...), condition=%wide.region_17.18_spmd.clone, body=%wide.region_16.17_spmd.clone.sunk | while | flops 1891107328 | bytes 13656793 | solution.py:236
  630.0 14.3 %sine_multiply_fusion = f32[1024,1,128,2]{0,3,2,1:T(2,128)S(1)} fusion(f32[1024,1,128,2]{0,3,2,1:T(2,128)S(1)} %reshape.491, f32[1024]{0:T(1024)S(1)} %subtract_convert_fusion, f32[128]{0:T(128)S(1)} %multiply_exponential_fusion), kind=kLoop, calls=%fused_computation.136 | loop fusion | flops 524288 | bytes 2101760 | tf_op jit(solution)/shard_map/transpose(jvp())/mul | solution.py:60
  664.4 6.1 convolution_convert_fusion.3
  685.5 6.0 fusion.106
  691.5 5.6 fusion.82
  697.1 9.5 add_convert_fusion
  711.2 119.5 %psum.101 = bf16[512]{0:T(512)(128)(2,1)S(1)} all-reduce(bf16[512]{0:T(512)(128)(2,1)S(1)} %get-tuple-element.310), channel_id=1, replica_groups=mesh['dp'=16,'mp_0'=2,'mp_1'=4] {'dp'}, use_global_device_ids=true, to_apply=%region_36.37 | all-reduce | flops 512 | bytes 2048 | tf_op jit(solution)/shard_map/psum | solution.py:275
  838.2 179.1 %all-reduce.4 = (f32[2048]{0:T(1024)}, f32[2048]{0:T(1024)}, f32[2048]{0:T(1024)}, f32[2048]{0:T(1024)}, f32[2048]{0:T(1024)}) all-reduce(f32[2048]{0:T(1024)S(1)} %get-tuple-element.255, f32[2048]{0:T(1024)S(1)} %get-tuple-element.251, ...), channel_id=1, replica_groups=mesh['dp'=16,'mp_0'=2,'mp_1'=4] {'dp','mp_0','mp_1'}, use_global_device_ids=true, to_apply=%region_22.23 | all-reduce | flops 10240 | bytes 81920 | tf_op jit(solution)/shard_map/psum | solution.py:265
  (238 shorter events, 178.3 us)
Async XLA Ops:
  7.2 356.3 %copy-start = (bf16[512,2048]{1,0:T(8,128)(2,1)S(1)}, bf16[512,2048]{1,0:T(8,128)(2,1)}, u32[]{:S(2)}) copy-start(bf16[512,2048]{1,0:T(8,128)(2,1)} %param.34) | copy-start | bytes 6291460
  7.2 6.4 copy-start.50
  7.2 61.5 %copy-start.31 = (bf16[2048,256]{1,0:T(8,128)(2,1)S(1)}, bf16[2048,256]{1,0:T(8,128)(2,1)}, u32[]{:S(2)}) copy-start(bf16[2048,256]{1,0:T(8,128)(2,1)} %param.26) | copy-start | bytes 3145732
  7.2 61.5 %all-gather.7.cloned.1.call-start = ((), (), s32[]{:S(2)}) async-start(), calls=%async_computation.4 | async-start | bytes 4718592 | tf_op jit(solution)/shard_map/all_gather | solution.py:138
  13.3 219.2 %reduce-scatter.4.cloned.1.call-start = ((), (), s32[]{:S(2)}) async-start(), calls=%async_computation.5 | async-start | bytes 9437184 | tf_op jit(solution)/shard_map/reduce_scatter | solution.py:169
  124.7 9.5 copy-start.3
  124.7 9.5 copy-start.9
  127.3 7.9 copy-start.48
  140.8 93.5 %copy-start.34 = (f32[2048]{0:T(1024)S(1)}, f32[2048]{0:T(1024)}, u32[]{:S(2)}) copy-start(f32[2048]{0:T(1024)} %param.30) | copy-start | bytes 24580
  140.8 93.5 %copy-start.37 = (f32[2048]{0:T(1024)S(1)}, f32[2048]{0:T(1024)}, u32[]{:S(2)}) copy-start(f32[2048]{0:T(1024)} %param.31) | copy-start | bytes 24580
  140.8 117.2 %all-gather.15.cloned.1.call-start = ((), (), s32[]{:S(2)}) async-start(), calls=%async_computation.11 | async-start | bytes 1572864 | tf_op jit(solution)/shard_map/all_gather | solution.py:28
  235.4 73.6 %all-gather.9.cloned.1.call-start = ((), (), s32[]{:S(2)}) async-start(), calls=%async_computation.6 | async-start | bytes 5242880 | tf_op jit(solution)/shard_map/all_gather | solution.py:28
  258.0 105.5 %all-gather.11.cloned.1.call-start = ((), (), s32[]{:S(2)}) async-start(), calls=%async_computation.8 | async-start | bytes 4718592 | tf_op jit(solution)/shard_map/all_gather | solution.py:191
  258.6 224.3 %reduce-scatter.8.cloned.1.call-start = ((), (), s32[]{:S(2)}) async-start(), calls=%async_computation.9 | async-start | bytes 9437184 | tf_op jit(solution)/shard_map/reduce_scatter | solution.py:198
  313.7 49.9 %copy-start.41 = (f32[512]{0:T(512)S(1)}, f32[512]{0:T(512)}, u32[]{:S(2)}) copy-start(f32[512]{0:T(512)} %param.33) | copy-start | bytes 6148
  363.5 22.0 %copy-start.47 = (bf16[2048,512]{1,0:T(8,128)(2,1)S(1)}, bf16[2048,512]{1,0:T(8,128)(2,1)}, u32[]{:S(2)}) copy-start(bf16[2048,512]{1,0:T(8,128)(2,1)} %param.32) | copy-start | bytes 6291460
  391.2 146.6 %reduce-scatter.6.cloned.1.call-start = ((), (), s32[]{:S(2)}) async-start(), calls=%async_computation.7 | async-start | bytes 4718592 | tf_op jit(solution)/shard_map/reduce_scatter | solution.py:181
  399.5 138.3 %copy-start.38 = (f32[2048]{0:T(1024)S(1)}, f32[2048]{0:T(1024)}, u32[]{:S(2)}) copy-start(f32[2048]{0:T(1024)} %param.35) | copy-start | bytes 24580
  399.5 193.5 %all-gather.13.cloned.1.call-start = ((), (), s32[]{:S(2)}) async-start(), calls=%async_computation.10 | async-start | bytes 4718592 | tf_op jit(solution)/shard_map/all_gather | solution.py:204
  484.5 55.9 %copy-start.11 = (bf16[128,2048]{1,0:T(8,128)(2,1)S(1)}, bf16[128,2048]{1,0:T(8,128)(2,1)}, u32[]{:S(2)}) copy-start(bf16[128,2048]{1,0:T(8,128)(2,1)} %param.21) | copy-start | bytes 1572868
  541.4 476.0 %all-reduce.8.cloned.1.call-start = ((), (), s32[]{:S(2)}) async-start(), calls=%async_computation.12 | async-start | bytes 25165824 | tf_op jit(solution)/shard_map/psum | solution.py:269
  593.0 6.9 copy-start.8
  593.0 6.9 copy-start.18
  706.7 124.7 %all-to-all-start = ((bf16[8,128,2048]{2,1,0:T(8,128)(2,1)}), bf16[8,128,2048]{2,1,0:T(8,128)(2,1)}, u32[]{:S(2)}, u32[]{:S(2)}) async-start(bf16[8,128,2048]{2,1,0:T(8,128)(2,1)} %bitcast.213), calls=%async_computation.3 | async-start | bytes 8388608 | tf_op jit(solution)/shard_map/all_to_all | solution.py:47
  (41 other events, 130.3 us)
Sparse Core Ops, SparseCore 0:
  13.4 55.2 all-gather.6
  140.9 91.4 reduce-scatter.3
  235.5 22.4 all-gather.14
  259.5 49.4 all-gather.8
  310.5 52.9 all-gather.10
  391.3 91.4 reduce-scatter.7
  485.8 51.9 reduce-scatter.5
  541.5 51.4 all-gather.12
  682.9 329.6 all-reduce.7
where the time goes:
time: 1050 us; the launch traced here: 1040 us
  waiting for transfers between devices  444 us (42%)
  blocking collectives  299 us (28%)
  matrix products  145 us (14%)
  other arithmetic  89.1 us (8%)
  local copies, waits for them, and re-layouts  38.4 us (4%)
  between operations  14.9 us (1%)
    psum x1, blocking collectives, local(): lax.psum((grad_ln1_gain, grad_ln1_bias, grad_ln2_gain, grad_ln2_bias, gra...  179 us
    psum x1, blocking collectives, local(): lax.psum(grad_b_up.astype(jnp.bfloat16), 'dp').astype(jnp.float32)  120 us
    reduce_scatter x1, waiting for transfers between devices, local(): lax.psum_scatter(jnp.dot(gated, w_out, preferred_element_type=jnp.float32...  91.6 us
    reduce_scatter x1, waiting for transfers between devices, local(): lax.psum_scatter(contract_cols(grad_pre, w_up), MP, scatter_dimension=0,...  83.3 us
    all_gather x2, waiting for transfers between devices, stacked_from(): pieces = lax.all_gather(pieces, axes[k], axis=0, tiled=True)  72.9 us
    dot_general x7, matrix products, contract_cols(): lax.dot_general(left_side, right_side, (((1,), (1,)), ((), ())), preferre...  57.4 us
    all_gather x1, waiting for transfers between devices, local(): gathered = lax.all_gather(normed, MP, axis=0, tiled=True)  54.7 us
    reduce_scatter x1, waiting for transfers between devices, local(): lax.psum_scatter(jnp.dot(hidden, w_down, preferred_element_type=jnp.float...  53.3 us
  transfers between devices with their start and end apart: 10, of which 8 were waited for; matrix products, arithmetic and copies ran while one was open for 5% of the time, Pallas kernels for 0%

commit v1 on v0

v1 whole, which is shorter than its diff:
```python
import functools
import math

import jax
import jax.numpy as jnp
import numpy as np
from jax import lax
from jax.experimental import pallas as pl
from jax.experimental.pallas import tpu as pltpu
from jax.sharding import Mesh
from jax.sharding import PartitionSpec as P

DK = 256
DV = 512
AXES = ("x", "yh", "c", "yl", "z")
DP = ("x", "yh", "c")
MP = ("yl", "z")
BF = jnp.bfloat16
F32 = jnp.float32
MIB = 1024 * 1024

norm_eps = 1e-05
group_eps = 1.0

WAVE_A = ((0, 0), (1, 0), (-1, 0), (0, 1))
WAVE_B = ((2, 0), (1, 1), (-1, 1), (2, 1))
ORDER = WAVE_A + WAVE_B


def after(value, *others):
    return lax.optimization_barrier((value, *others))[0]


class Line:
    def __init__(self):
        self.last = ()

    def hold(self, value):
        return after(value, *self.last) if self.last else value

    def done(self, value):
        self.last = (value,)
        return value

    def wait(self, *values):
        self.last = (*self.last, *values)


def plus(*terms):
    return functools.reduce(lambda u, v: u + v, [t.astype(F32) for t in terms])


def shifted(value, axis, step):
    size = lax.axis_size(axis)
    return lax.ppermute(value, axis, [((i + step) % size, i) for i in range(size)])


def by_sides(value, axis, way):
    size = lax.axis_size(axis)
    names = ("x", "c") if axis == "x" else ("c", axis)

    def flat(c, i):
        return i * 2 + c if axis == "x" else c * size + i

    pairs = []
    for c, step in ((0, way), (1, -way)):
        for i in range(size):
            pairs.append((flat(c, (i + step) % size), flat(c, i)))
    return lax.ppermute(value, names, pairs)


def across(value, axis):
    return by_sides(value, axis, 1)


def across_back(value, axis):
    return by_sides(value, axis, -1)


class Gather:
    def __init__(self, own):
        self.got = got = {(0, 0): own}
        got[1, 0] = shifted(own, "z", 1)
        got[-1, 0] = shifted(own, "z", -1)
        got[0, 1] = shifted(own, "yl", 1)

    def second(self, line):
        got = self.got
        line.wait(got[0, 1], got[1, 0], got[-1, 0])
        got[2, 0] = across(line.done(by_core(line.hold(got[1, 0]), got[-1, 0])), "z")
        got[1, 1] = shifted(got[0, 1], "z", 1)
        got[-1, 1] = shifted(got[0, 1], "z", -1)
        got[2, 1] = shifted(got[2, 0], "yl", 1)

    def wave(self, places):
        return [self.got[p] for p in places]


class LateGather(Gather):
    def __init__(self, own):
        self.got = {(0, 0): own, (0, 1): shifted(own, "yl", 1)}

    def sides(self, line):
        got = self.got
        own, other = line.hold(got[0, 0]), line.hold(got[0, 1])
        got[1, 0] = shifted(own, "z", 1)
        got[-1, 0] = shifted(own, "z", -1)
        got[1, 1] = shifted(other, "z", 1)
        got[-1, 1] = shifted(other, "z", -1)

    def second(self, line):
        got = self.got
        got[2, 0] = across(line.done(by_core(line.hold(got[1, 0]), got[-1, 0])), "z")

    def third(self, line):
        self.got[2, 1] = shifted(line.hold(self.got[2, 0]), "yl", 1)


class Scatter:
    def __init__(self, part):
        self.part = part
        self.far = shifted(part[2, 1], "yl", 1)
        self.up = shifted(part[1, 1], "z", -1)
        self.down = shifted(part[-1, 1], "z", 1)

    def relay(self, line):
        line.wait(self.far)
        self.passed = across_back(line.done(added(line.hold(self.part[2, 0]), self.far)), "z")

    def side(self, line):
        part = self.part
        line.wait(self.up, self.down)
        self.other = shifted(line.done(added(line.hold(part[0, 1]), self.up, self.down)), "yl", 1)

    def near(self, line):
        part = self.part
        line.wait(self.passed)
        up, down = pair(line.hold(part[1, 0]), part[-1, 0], self.passed)
        line.done(up)
        self.near_up = shifted(up, "z", -1)
        self.near_down = shifted(down, "z", 1)

    def terms(self):
        return [self.part[0, 0], self.other, self.near_up, self.near_down]


class Summed:
    def __init__(self, value, axes):
        self.value, self.left, self.come = value, [], None
        for axis in axes:
            size = lax.axis_size(axis)
            mates = ((1, 0),) if size == 2 else ((1, 0, 3, 2), (3, 2, 1, 0))
            self.left += [(axis, [(i, mate[i]) for i in range(size)]) for mate in mates]

    def step(self, line):
        if self.come is not None:
            line.wait(self.come)
            self.value = line.done(line.hold(self.value) + self.come)
            self.come = None
        if self.left:
            axis, pairs = self.left.pop(0)
            self.come = lax.ppermute(self.value, axis, pairs)


def dot_nn(a, b):
    return jnp.dot(a, b, preferred_element_type=F32)


def dot_nt(a, b):
    return lax.dot_general(a, b, (((1,), (1,)), ((), ())), preferred_element_type=F32)


def dot_tn(a, b):
    return lax.dot_general(a, b, (((0,), (0,)), ((), ())), preferred_element_type=F32)


def like(shape, dtype):
    return jax.ShapeDtypeStruct(shape, dtype)


def in_hbm(value):
    return pltpu.with_memory_space_constraint(value, pltpu.HBM)


NO_COST = pl.CostEstimate(flops=0, bytes_accessed=0, transcendentals=0)


def simple(body, outs, args, name, vmem, scalars=0, scratch=()):
    in_specs = [pl.BlockSpec(memory_space=pltpu.SMEM)] * scalars
    in_specs += [pl.BlockSpec(memory_space=pltpu.VMEM)] * (len(args) - scalars)
    return pl.pallas_call(
        body,
        in_specs=in_specs,
        out_specs=[pl.BlockSpec(memory_space=pltpu.VMEM)] * len(outs),
        out_shape=outs,
        scratch_shapes=list(scratch),
        compiler_params=pltpu.CompilerParams(vmem_limit_bytes=vmem * MIB),
        cost_estimate=NO_COST,
        name=name,
    )(*args)


def centred(values):
    centre = values - jnp.mean(values, -1, keepdims=True)
    scale = lax.rsqrt(jnp.mean(centre * centre, -1, keepdims=True) + norm_eps)
    return centre * scale, scale


def norm_kernel(inputs, gain, bias, out):
    xhat, _ = centred(inputs[...].astype(F32))
    out[...] = (xhat * gain[...] + bias[...]).astype(BF)


def norm(inputs, gain, bias):
    return simple(norm_kernel, [like(inputs.shape, BF)], [inputs, gain, bias], "norm", 6)[0]


def middle_kernel(inputs, own, side, up, down, gain, bias, middle, out):
    value = inputs[...].astype(F32) + plus(own[...], side[...], up[...], down[...])
    middle[...] = value
    xhat, _ = centred(value)
    out[...] = (xhat * gain[...] + bias[...]).astype(BF)


def middle_norm(inputs, terms, gain, bias):
    outs = [like(inputs.shape, F32), like(inputs.shape, BF)]
    return simple(middle_kernel, outs, [inputs, *terms, gain, bias], "middle", 10)


def norm_back(xhat, scale, grad, gain):
    e = grad * gain
    return scale * (e - jnp.mean(e, -1, keepdims=True) - xhat * jnp.mean(e * xhat, -1, keepdims=True))


def middle_back_kernel(middle, cot, own, side, up, down, gain, grad, low, sums):
    xhat, scale = centred(middle[...])
    term = plus(own[...], side[...], up[...], down[...])
    dy = cot[...].astype(F32)
    value = dy + norm_back(xhat, scale, term, gain[...])
    grad[...] = value
    low[...] = value.astype(BF)
    sums[0:1, :] = jnp.sum(term * xhat, 0, keepdims=True)
    sums[1:2, :] = jnp.sum(term, 0, keepdims=True)
    sums[2:3, :] = jnp.sum(dy, 0, keepdims=True)


def middle_back(middle, cot, terms, gain):
    outs = [like(middle.shape, F32), like(middle.shape, BF), like((3, middle.shape[1]), F32)]
    return simple(middle_back_kernel, outs, [middle, cot, *terms, gain], "middle_back", 12)


def input_back_kernel(inputs, middle_grad, own, side, up, down, gain, grad, sums):
    xhat, scale = centred(inputs[...].astype(F32))
    term = plus(own[...], side[...], up[...], down[...])
    grad[...] = middle_grad[...] + norm_back(xhat, scale, term, gain[...])
    sums[0:1, :] = jnp.sum(term * xhat, 0, keepdims=True)
    sums[1:2, :] = jnp.sum(term, 0, keepdims=True)


def input_back(inputs, middle_grad, terms, gain):
    outs = [like(inputs.shape, F32), like((2, inputs.shape[1]), F32)]
    return simple(input_back_kernel, outs, [inputs, middle_grad, *terms, gain], "input_back", 12)


def angle_tables(rows, blocks):
    half = DK // 2
    frequency = np.repeat(np.exp(-math.log(10000.0) * np.arange(half) / max(half - 1, 1)), 2)
    inner = np.arange(rows)[:, None] * frequency[None, :]
    outer = (np.arange(blocks) * rows)[:, None] * frequency[None, :]
    return [jnp.asarray(t, F32) for t in (np.cos(inner), np.sin(inner), np.cos(outer), np.sin(outer))]


def turn(values, cosine, sine, back):
    lane = lax.broadcasted_iota(jnp.int32, values.shape, 1)
    even = lane % 2 == 0
    if back:
        turned = values * sine
        return values * cosine + jnp.where(even, pltpu.roll(turned, DK - 1, 1), -pltpu.roll(turned, 1, 1))
    return values * cosine + jnp.where(even, -pltpu.roll(values, DK - 1, 1), pltpu.roll(values, 1, 1)) * sine


def block_angles(marks, number, tables):
    cos_in, sin_in, cos_out, sin_out = tables
    rows = cos_in.shape[0]
    block, first, second = marks[number], marks[8], marks[9]

    def joined(outer, inner):
        co, so = cos_out[pl.ds(outer, 1), :], sin_out[pl.ds(outer, 1), :]
        ci, si = cos_in[inner, :], sin_in[inner, :]
        return ci * co - si * so, si * co + ci * so

    cosine, sine = joined(block, slice(0, rows))
    cos_one, sin_one = joined(0, pl.ds(lax.rem(first, rows), 1))
    last = jnp.minimum(lax.div(second, rows), cos_out.shape[0] - 1)
    cos_two, sin_two = joined(last, pl.ds(lax.rem(second, rows), 1))
    token = block * rows + lax.broadcasted_iota(jnp.int32, (rows, 1), 0)
    back_cos = jnp.where(token >= second, cos_two, jnp.where(token >= first, cos_one, 1.0))
    back_sin = jnp.where(token >= second, sin_two, jnp.where(token >= first, sin_one, 0.0))
    return cosine * back_cos + sine * back_sin, sine * back_cos - cosine * back_sin


def pack(blocks, out):
    rows = blocks[0].shape[0]
    for n, block in enumerate(blocks):
        out[n * rows : (n + 1) * rows, :] = block[...]


def unpack(value, first, outs):
    rows = outs[0].shape[0]
    for n in range(value.shape[0] // rows):
        out = outs[first + n]
        out[...] = value[n * rows : (n + 1) * rows, :].astype(out.dtype)


def heads_kernel(marks, b0, b1, b2, b3, wq, wk, wv, wg, ci, si, co, so, x, qr, kr, vb, gate, *, first):
    pack((b0, b1, b2, b3), x)
    rows = b0.shape[0]
    q = dot_nn(x[...], wq[...])
    k = dot_nn(x[...], wk[...])
    for n in range(4):
        cosine, sine = block_angles(marks, first + n, (ci, si, co, so))
        at = slice(n * rows, (n + 1) * rows)
        qr[at, :] = turn(q[at, :], cosine, sine, False).astype(BF)
        kr[at, :] = turn(k[at, :], cosine, sine, False).astype(BF)
    vb[...] = dot_nn(x[...], wv[...]).astype(BF)
    gate[...] = dot_nn(x[...], wg[...])


def heads(marks, blocks, weights, tables, first):
    rows, width = blocks[0].shape
    n = 4 * rows
    outs = [like((n, width), BF), like((n, DK), BF), like((n, DK), BF), like((n, DV), BF), like((n, DV), F32)]
    return simple(
        functools.partial(heads_kernel, first=first), outs, [marks, *blocks, *weights, *tables], "heads", 20, 1
    )


def places_of(marks, first, rows, axis):
    shape = (rows, 1) if axis == 0 else (1, rows)
    lane = lax.broadcasted_iota(jnp.int32, shape, axis)
    return jnp.concatenate([marks[first + n] * rows + lane for n in range(4)], axis)


def row_marks(marks, decay, first, rows):
    place = places_of(marks, first, rows, 0)
    low = jnp.where(place >= marks[9], marks[9], jnp.where(place >= marks[8], marks[8], 0))
    return place, low, jnp.exp(place.astype(F32) * decay[0])


def col_marks(marks, decay, first, rows):
    place = places_of(marks, first, rows, 1)
    return place, jnp.exp(place.astype(F32) * -decay[0])


def mask_of(at, row, col):
    place, low, fade = (m[at, :] for m in row)
    seen = (col[0] <= place) & (col[0] >= low)
    return jnp.where(seen, fade * col[1], 0.0)


def retain_kernel(
    marks, decay, qr, kr_a, kr_b, vb_a, vb_b, gate, w_out, ret, gated, *outs, first
):
    half = kr_a.shape[0]
    tile = qr.shape[0] // 2
    rows = half // 4
    row = row_marks(marks, decay, first, rows)
    cols = [col_marks(marks, decay, n, rows) for n in (0, 4)]
    for i in range(2):
        at = slice(i * tile, (i + 1) * tile)
        out = None
        for k, v, col in ((kr_a, vb_a, cols[0]), (kr_b, vb_b, cols[1])):
            scores = (dot_nt(qr[at, :], k[...]) * mask_of(at, row, col)).astype(BF)
            term = dot_nn(scores, v[...])
            out = term if out is None else out + term
        ret[at, :] = out
        scale = lax.rsqrt(jnp.mean(out * out, -1, keepdims=True) + group_eps)
        g = gate[at, :]
        low = (g / (1.0 + jnp.exp(-g)) * out * scale).astype(BF)
        gated[at, :] = low
        unpack(dot_nn(low, w_out[...]), i * 2, outs)


def block_outs(places, shape):
    return [like(shape, F32 if p == (0, 0) else BF) for p in places]


def retain(marks, decay, places, q, ks, vs, gate, w_out):
    rows = q.shape[0]
    outs = [like((rows, DV), F32), like((rows, DV), BF)] + block_outs(places, (rows // 4, w_out.shape[1]))
    body = functools.partial(retain_kernel, first=ORDER.index(places[0]))
    got = simple(body, outs, [marks, decay, q, *ks, *vs, gate, w_out], "retain", 16, 2)
    return got[0], got[1], dict(zip(places, got[2:]))


def hidden_grad_kernel(b0, b1, b2, b3, w_down, packed, out):
    pack((b0, b1, b2, b3), packed)
    out[...] = dot_nt(packed[...], w_down[...])


def hidden_grad(blocks, w_down):
    rows, width = blocks[0].shape
    outs = [like((4 * rows, width), BF), like((4 * rows, w_down.shape[0]), F32)]
    return simple(hidden_grad_kernel, outs, [*blocks, w_down], "hidden_grad", 12)


def feed_kernel(b0, b1, b2, b3, w_up, b_up, dh, packed, hidden, dpre, bias_sum, *outs):
    pack((b0, b1, b2, b3), packed)
    tile = packed.shape[0] // 2
    total = None
    for i in range(2):
        at = slice(i * tile, (i + 1) * tile)
        pre = dot_nn(packed[at, :], w_up[...]) + b_up[...]
        below = 0.5 * (1.0 + lax.erf(pre * (1.0 / math.sqrt(2.0))))
        hidden[at, :] = (pre * below).astype(BF)
        slope = below + pre * jnp.exp(-0.5 * pre * pre) * (1.0 / math.sqrt(2.0 * math.pi))
        low = (dh[at, :] * slope).astype(BF)
        dpre[at, :] = low
        column = jnp.sum(low.astype(F32), 0, keepdims=True)
        total = column if total is None else total + column
        unpack(dot_nt(low, w_up[...]), i * 2, outs)
    bias_sum[...] = total


def feed(places, blocks, w_up, b_up, dh):
    rows, width = blocks[0].shape
    hidden = w_up.shape[1]
    n = 4 * rows
    outs = [like((n, width), BF), like((n, hidden), BF), like((n, hidden), BF), like((1, hidden), F32)]
    outs += block_outs(places, (rows, width))
    got = simple(feed_kernel, outs, [*blocks, w_up, b_up, dh], "feed", 16)
    return *got[:4], dict(zip(places, got[4:]))


def feed_out_kernel(hidden, w_down, *outs):
    tile = hidden.shape[0] // 2
    for i in range(2):
        unpack(dot_nn(hidden[i * tile : (i + 1) * tile, :], w_down[...]), i * 2, outs)


def feed_out(places, hidden, w_down):
    outs = block_outs(places, (hidden.shape[0] // 4, w_down.shape[1]))
    return dict(zip(places, simple(feed_out_kernel, outs, [hidden, w_down], "feed_out", 10)))


def gate_back_kernel(b0, b1, b2, b3, w_out, ret, gate, packed, dret, dgate):
    pack((b0, b1, b2, b3), packed)
    tile = packed.shape[0] // 2
    for i in range(2):
        at = slice(i * tile, (i + 1) * tile)
        dgt = dot_nt(packed[at, :], w_out[...])
        g = gate[at, :]
        out = ret[at, :]
        sig = 1.0 / (1.0 + jnp.exp(-g))
        scale = lax.rsqrt(jnp.mean(out * out, -1, keepdims=True) + group_eps)
        y = out * scale
        dgate[at, :] = (dgt * y * (sig * (1.0 + g * (1.0 - sig)))).astype(BF)
        e = dgt * (g * sig)
        dret[at, :] = (scale * (e - y * jnp.mean(e * y, -1, keepdims=True))).astype(BF)


def gate_back(blocks, w_out, ret, gate):
    rows, width = blocks[0].shape
    outs = [like((4 * rows, width), BF), like((4 * rows, DV), BF), like((4 * rows, DV), BF)]
    return simple(gate_back_kernel, outs, [*blocks, w_out, ret, gate], "gate_back", 16)


def retain_back_kernel(
    marks, decay, qr_a, qr_b, kr_a, kr_b, vb_a, vb_b, dret_a, dret_b, ci, si, co, so,
    grads_a, grads_b, dk_sum, dv_sum,
):
    half = qr_a.shape[0]
    tile = half // 2
    rows = ci.shape[0]
    tables = (ci, si, co, so)

    def turned(value, block):
        cosine, sine = block_angles(marks, block, tables)
        return turn(value, cosine, sine, True).astype(BF)

    row_parts = [row_marks(marks, decay, n, rows) for n in (0, 4)]
    col_parts = [col_marks(marks, decay, n, rows) for n in (0, 4)]
    for i in range(4):
        q_ref, dret_ref, grads = (qr_a, dret_a, grads_a) if i < 2 else (qr_b, dret_b, grads_b)
        at = slice(i % 2 * tile, (i % 2 + 1) * tile)
        q = q_ref[at, :]
        dret = dret_ref[at, :]
        dq = None
        for j, (k, v) in enumerate(((kr_a, vb_a), (kr_b, vb_b))):
            cols = slice(j * half, (j + 1) * half)
            mask = mask_of(at, row_parts[i // 2], col_parts[j])
            scores = (dot_nt(q, k[...]) * mask).astype(BF)
            raw = (dot_nt(dret, v[...]) * mask).astype(BF)
            term = dot_nn(raw, k[...])
            dq = term if dq is None else dq + term
            if i == 0:
                dk_sum[cols, :] = dot_tn(raw, q)
                dv_sum[cols, :] = dot_tn(scores, dret)
            else:
                dk_sum[cols, :] += dot_tn(raw, q)
                dv_sum[cols, :] += dot_tn(scores, dret)
        for n in range(tile // rows):
            grads[i % 2 * tile + n * rows : i % 2 * tile + (n + 1) * rows, 0:DK] = turned(
                dq[n * rows : (n + 1) * rows, :], i * (tile // rows) + n
            )
    for j, grads in enumerate((grads_a, grads_b)):
        for n in range(half // rows):
            at = slice(j * half + n * rows, j * half + (n + 1) * rows)
            grads[n * rows : (n + 1) * rows, DK : 2 * DK] = turned(dk_sum[at, :], j * (half // rows) + n)
        grads[:, 2 * DK : 2 * DK + DV] = dv_sum[j * half : (j + 1) * half, :].astype(BF)


def retain_back(marks, decay, qs, ks, vs, drets, tables):
    half = qs[0].shape[0]
    outs = [like((half, 2 * DK + DV), BF)] * 2
    scratch = [pltpu.VMEM((2 * half, DK), F32), pltpu.VMEM((2 * half, DV), F32)]
    args = [marks, decay, *qs, *ks, *vs, *drets, *tables]
    return simple(retain_back_kernel, outs, args, "retain_back", 18, 2, scratch)


def heads_back_kernel(dqkv, dgate, wq, wk, wv, wg, *outs):
    tile = dqkv.shape[0] // 2
    for i in range(2):
        at = slice(i * tile, (i + 1) * tile)
        total = dot_nt(dqkv[at, 0:DK], wq[...]) + dot_nt(dqkv[at, DK : 2 * DK], wk[...])
        total = total + dot_nt(dqkv[at, 2 * DK : 2 * DK + DV], wv[...]) + dot_nt(dgate[at, :], wg[...])
        unpack(total, i * 2, outs)


def heads_back(places, dqkv, dgate, weights):
    outs = block_outs(places, (dqkv.shape[0] // 4, weights[0].shape[0]))
    return dict(zip(places, simple(heads_back_kernel, outs, [dqkv, dgate, *weights], "heads_back", 18)))


def added_kernel(*refs):
    refs[-1][...] = plus(*[r[...] for r in refs[:-1]]).astype(BF)


def added(*terms):
    return simple(added_kernel, [like(terms[0].shape, BF)], list(terms), "added", 6)[0]


def chosen_kernel(core, first, second, out):
    @pl.when(core[0] == 0)
    def _():
        out[...] = first[...]

    @pl.when(core[0] != 0)
    def _():
        out[...] = second[...]


def by_core(first, second):
    core = lax.axis_index("c").astype(jnp.int32)[None]
    return simple(chosen_kernel, [like(first.shape, first.dtype)], [core, first, second], "chosen", 6, 1)[0]


def pair_kernel(core, up, down, passed, new_up, new_down):
    first = core[0] == 0
    value = passed[...].astype(F32)
    new_up[...] = (up[...].astype(F32) + jnp.where(first, value, 0.0)).astype(BF)
    new_down[...] = (down[...].astype(F32) + jnp.where(first, 0.0, value)).astype(BF)


def pair(up, down, passed):
    core = lax.axis_index("c").astype(jnp.int32)[None]
    return simple(pair_kernel, [like(up.shape, BF)] * 2, [core, up, down, passed], "pair", 6, 1)


def near_kernel(near, passed, out):
    rows = passed.shape[0]
    out[0:rows, :] = plus(near[0:rows, :], passed[...]).astype(BF)
    out[rows : 2 * rows, :] = near[rows : 2 * rows, :]


def quarter_kernel(own, come, swapped, out):
    rows = own.shape[0]
    out[...] = plus(own[...], come[0:rows, :], swapped[rows : 2 * rows, :]).astype(BF)


def both_kernel(first, second, out):
    rows = first.shape[0]
    out[0:rows, :] = first[...]
    out[rows : 2 * rows, :] = second[...]


def upper_kernel(both, out):
    out[...] = both[0 : out.shape[0], :]


def weight_kernel(places, *refs, counts, rest):
    refs = list(refs)
    lefts, rights = [], []
    for count in counts:
        lefts.append([refs.pop(0) for _ in range(count)])
        rights.append([refs.pop(0) for _ in range(count)])
    more = refs.pop(0) if rest else None
    step = pl.program_id(0)
    at = 0
    parts = []
    for left, right in zip(lefts, rights):
        total = functools.reduce(lambda u, v: u + v, [dot_tn(l[...], r[...]) for l, r in zip(left, right)])
        width = total.shape[1]
        if rest:
            total = total + more[:, at : at + width].astype(F32)
        parts.append((at, width, total.astype(BF)))
        at += width
    if not rest:
        for at, width, total in parts:
            refs[0][:, at : at + width] = total
        return
    two, near, own = refs
    rows = two.shape[0]
    for k, (out, first) in enumerate(((two, 0), (near, 0), (near, rows), (own, 0))):

        @pl.when(step == k)
        def _(out=out, first=first):
            for at, width, total in parts:
                out[first : first + rows, at : at + width] = total


def weight_parts(pairs, places, first, more):
    piece = pairs[0][0][0].shape[1] // 8
    specs, args, columns = [], [], 0
    for lefts, rights in pairs:
        for left in lefts:
            specs.append(pl.BlockSpec((left.shape[0], piece), lambda i, places: (0, places[first + i])))
            args.append(left)
        for right, shape, at in rights:
            specs.append(pl.BlockSpec(shape, lambda i, places, at=at: at))
            args.append(right)
        columns += rights[0][1][1]
    if more is None:
        out_specs = pl.BlockSpec((piece, columns), lambda i, places: (i, 0))
        out_shape = like((4 * piece, columns), BF)
    else:
        specs.append(pl.BlockSpec((piece, columns), lambda i, places: (i, 0)))
        args.append(more)
        out_shape = [like((piece * n, columns), BF) for n in (1, 2, 1)]
        out_specs = [pl.BlockSpec(o.shape, lambda i, places: (0, 0)) for o in out_shape]
    return pl.pallas_call(
        functools.partial(weight_kernel, counts=[len(lefts) for lefts, _ in pairs], rest=more is not None),
        grid_spec=pltpu.PrefetchScalarGridSpec(num_scalar_prefetch=1, grid=(4,), in_specs=specs, out_specs=out_specs),
        out_shape=out_shape,
        compiler_params=pltpu.CompilerParams(vmem_limit_bytes=16 * MIB),
        cost_estimate=NO_COST,
        name="weight_parts",
    )(places, *args)


def piece_places():
    size = lax.axis_size("x")
    xi = lax.axis_index("x")

    def number(half, step):
        return half * size + (xi + step + size) % size

    def kept(core):
        way = 1 - 2 * core
        return [number(core, 2), number(core, way), number(1 - core, way), number(core, 0)]

    core = lax.axis_index("c")
    way = 1 - 2 * core
    last = [number(core, 0), number(1 - core, 0), number(core, -way), number(1 - core, -way)]
    last += [number(1 - core, way), number(core, way), number(core, 2), number(1 - core, 2)]
    return [jnp.stack(p).astype(jnp.int32) for p in (kept(1 - core) + kept(core), last)]


def holding(line, pairs):
    (lefts, rights), *more = pairs
    return [([line.hold(lefts[0]), *lefts[1:]], rights), *more]


class OverGroups:
    def __init__(self, places):
        self.places = places

    def send(self, line, pairs):
        self.pairs = pairs
        self.other = shifted(line.done(weight_parts(holding(line, pairs), self.places, 0, None)), "c", 1)

    def keep(self, line):
        line.wait(self.other)
        two, self.side, self.own = weight_parts(holding(line, self.pairs), self.places, 4, self.other)
        line.done(self.own)
        self.passed = across_back(two, "x")

    def near(self, line):
        line.wait(self.passed)
        shape = self.side.shape
        side = simple(near_kernel, [like(shape, BF)], [line.hold(self.side), self.passed], "near", 8)[0]
        self.come = across_back(line.done(side), "x")

    def half(self, line):
        line.wait(self.come)
        self.come = line.done(line.hold(self.come))
        self.swapped = shifted(self.come, "c", 1)

    def quarter(self, line):
        line.wait(self.swapped)
        args = [line.hold(self.own), self.come, self.swapped]
        self.mine = line.done(simple(quarter_kernel, [like(self.own.shape, BF)], args, "quarter", 8)[0])
        self.theirs = shifted(self.mine, "yh", 1)

    def whole(self, line):
        line.wait(self.theirs)
        self.mine = line.done(added(line.hold(self.mine), self.theirs))
        self.swapped = shifted(self.mine, "c", 1)

    def spread(self, line):
        line.wait(self.swapped)
        rows, width = self.mine.shape
        args = [line.hold(self.mine), self.swapped]
        self.both = line.done(simple(both_kernel, [like((2 * rows, width), BF)], args, "both", 8)[0])
        self.come = across_back(self.both, "x")

    def last(self, line):
        line.wait(self.come)
        upper = simple(upper_kernel, [like(self.mine.shape, BF)], [line.hold(self.come)], "upper", 6)[0]
        self.two = across_back(line.done(upper), "x")

    def swap(self, line):
        line.wait(self.two)
        come, two = line.hold(self.come), line.hold(self.two)
        self.moved = [shifted(come, "c", 1), shifted(two, "c", 1)]

    def pieces(self, line):
        line.wait(*self.moved)
        return [line.hold(self.both), self.come, self.moved[0], self.two, self.moved[1]]


def place_kernel(places, *refs, columns, turned, counts):
    step = pl.program_id(0)
    pieces, outs = refs[: len(counts)], refs[len(counts) :]
    first = 0
    for piece, count in zip(pieces, counts):

        @pl.when((step >= first) & (step < first + count))
        def _(piece=piece):
            at = 0
            for out, width, turn_it in zip(outs, columns, turned):
                value = piece[:, at : at + width].astype(F32)
                out[...] = value.T if turn_it else value
                at += width

        first += count


def placed(pieces, places, columns, turned):
    rows = min(p.shape[0] for p in pieces)
    counts = [p.shape[0] // rows for p in pieces]
    out_specs, out_shape, in_specs = [], [], []
    for width, turn_it in zip(columns, turned):
        if turn_it:
            out_specs.append(pl.BlockSpec((width, rows), lambda i, places: (0, places[i])))
            out_shape.append(jax.ShapeDtypeStruct((width, 8 * rows), F32))
        else:
            out_specs.append(pl.BlockSpec((rows, width), lambda i, places: (places[i], 0)))
            out_shape.append(jax.ShapeDtypeStruct((8 * rows, width), F32))
    first = 0
    for piece, count in zip(pieces, counts):
        in_specs.append(
            pl.BlockSpec((rows, piece.shape[1]), lambda i, places, f=first, n=count: (jnp.clip(i - f, 0, n - 1), 0))
        )
        first += count
    return pl.pallas_call(
        functools.partial(place_kernel, columns=columns, turned=turned, counts=counts),
        grid_spec=pltpu.PrefetchScalarGridSpec(
            num_scalar_prefetch=1, grid=(8,), in_specs=in_specs, out_specs=out_specs
        ),
        out_shape=out_shape,
        compiler_params=pltpu.CompilerParams(vmem_limit_bytes=16 * MIB),
        cost_estimate=NO_COST,
        name="placed",
    )(places, *pieces)


def local(
    tokens_in,
    cotangent,
    lengths,
    ln1_gain,
    ln1_bias,
    w_query,
    w_key,
    w_value,
    w_gate,
    w_out,
    ln2_gain,
    ln2_bias,
    w_up,
    b_up,
    w_down,
    b_down,
):
    rows = tokens_in.shape[0]
    half = rows * 4
    z_size = lax.axis_size("z")
    blocks = z_size * lax.axis_size("yl")
    zi = lax.axis_index("z")
    yi = lax.axis_index("yl")
    ends = jnp.cumsum(lengths[0])
    marks = [((yi + dy) % 2) * z_size + (zi + dz) % z_size for dz, dy in ORDER] + [ends[0], ends[1]]
    marks = jnp.stack([m.astype(jnp.int32) for m in marks])
    decay = jnp.log1p(-jnp.exp2(-5.0 - lax.axis_index(MP).astype(F32)))[None]
    tables = angle_tables(rows, blocks)
    places, final = piece_places()
    weights = (w_query, w_key, w_value, w_gate)
    heads_weights = tuple(in_hbm(w) for w in weights)
    gain_one, bias_one, gain_two, bias_two = (v[None, :] for v in (ln1_gain, ln1_bias, ln2_gain, ln2_bias))
    square = (half, DV)
    line = Line()

    xg = Gather(line.done(norm(tokens_in, gain_one, bias_one)))
    cg = LateGather(line.hold(cotangent))
    line.done(marks)
    xg.second(line)
    got = xg.got
    line.wait(got[2, 0], cg.got[0, 1])
    cg.sides(line)
    x_a, q_a, k_a, v_a, gate_a = heads(
        marks, [line.hold(got[0, 0]), got[1, 0], got[-1, 0], got[0, 1]], heads_weights, tables, 0
    )
    line.done(q_a)
    line.wait(got[1, 1], got[-1, 1], got[2, 1])
    x_b, q_b, k_b, v_b, gate_b = heads(
        marks, [line.hold(got[2, 0])] + xg.wave(WAVE_B[1:]), heads_weights, tables, 4
    )
    line.done(q_b)
    ks, vs = (k_a, k_b), (v_a, v_b)
    ret_b, gated_b, part_b = retain(marks, decay, WAVE_B, q_b, ks, vs, gate_b, w_out)
    line.done(gated_b)
    cot = cg.got
    line.wait(cot[1, 0], cot[-1, 0], cot[1, 1], cot[-1, 1])
    ret_a, gated_a, part_a = retain(marks, decay, WAVE_A, line.hold(q_a), ks, vs, gate_a, w_out)
    line.done(gated_a)
    rs = Scatter({**part_a, **part_b})
    rs.relay(line)
    rs.side(line)
    cg.second(line)
    rs.near(line)
    cot_a, dh_a = hidden_grad([line.hold(cot[0, 0])] + cg.wave(WAVE_A[1:]), w_down)
    line.done(dh_a)
    line.wait(cot[2, 0])
    cg.third(line)
    first, *others = rs.terms()
    line.wait(*others)
    middle, normed_two = middle_norm(tokens_in, [line.hold(first), *others], gain_two, bias_two)

    ng = Gather(line.done(normed_two))
    line.wait(cot[2, 1])
    cot_b, dh_b = hidden_grad([line.hold(cot[2, 0])] + cg.wave(WAVE_B[1:]), w_down)
    line.done(dh_b)
    ng.second(line)
    got = ng.got
    line.wait(got[2, 0])
    n_a, hid_a, dpre_a, bsum_a, part_a = feed(
        WAVE_A, [line.hold(got[0, 0]), got[1, 0], got[-1, 0], got[0, 1]], w_up, b_up[None, :], dh_a
    )
    line.done(bsum_a)
    line.wait(got[1, 1], got[-1, 1], got[2, 1])
    n_b, hid_b, dpre_b, bsum_b, part_b = feed(
        WAVE_B, [line.hold(got[2, 0])] + ng.wave(WAVE_B[1:]), w_up, b_up[None, :], dh_b
    )
    line.done(bsum_b)
    rs = Scatter({**part_a, **part_b})
    out_b = feed_out(WAVE_B, line.hold(hid_b), w_down)
    line.done(out_b[2, 1])
    out_a = feed_out(WAVE_A, line.hold(hid_a), w_down)
    line.done(out_a[0, 1])
    rs.relay(line)
    rs.side(line)
    feed_sums = OverGroups(places)
    feed_sums.send(
        line,
        [
            ([n_a, n_b], [(dpre_a, dpre_a.shape, (0, 0)), (dpre_b, dpre_b.shape, (0, 0))]),
            ([cot_a, cot_b], [(hid_a, hid_a.shape, (0, 0)), (hid_b, hid_b.shape, (0, 0))]),
        ],
    )
    rs.near(line)
    feed_sums.keep(line)
    first, *others = rs.terms()
    line.wait(*others)
    grad_middle, branch, early = middle_back(middle, cotangent, [line.hold(first), *others], gain_two)

    bg = Gather(line.done(branch))
    feed_sums.near(line)
    bg.second(line)
    got = bg.got
    line.wait(got[2, 0])
    br_a, dret_a, dgate_a = gate_back(
        [line.hold(got[0, 0]), got[1, 0], got[-1, 0], got[0, 1]], w_out, ret_a, gate_a
    )
    line.done(dret_a)
    feed_sums.half(line)
    feed_sums.quarter(line)
    line.wait(got[1, 1], got[-1, 1], got[2, 1])
    br_b, dret_b, dgate_b = gate_back([line.hold(got[2, 0])] + bg.wave(WAVE_B[1:]), w_out, ret_b, gate_b)
    line.done(dret_b)
    gate_sums = OverGroups(places)
    gate_sums.send(
        line,
        [
            ([x_a, x_b], [(dgate_a, square, (0, 0)), (dgate_b, square, (0, 0))]),
            ([br_a, br_b], [(gated_a, square, (0, 0)), (gated_b, square, (0, 0))]),
        ],
    )
    dqkv_a, dqkv_b = retain_back(marks, decay, (q_a, q_b), ks, vs, (line.hold(dret_a), dret_b), tables)
    line.done(dqkv_b)
    gate_sums.keep(line)
    feed_sums.whole(line)
    part_b = heads_back(WAVE_B, line.hold(dqkv_b), dgate_b, weights)
    line.done(part_b[2, 1])
    part_a = heads_back(WAVE_A, line.hold(dqkv_a), dgate_a, weights)
    line.done(part_a[0, 1])
    rs = Scatter({**part_a, **part_b})
    gate_sums.near(line)
    head_sums = OverGroups(places)
    head_sums.send(line, [([x_a, x_b], [(dqkv_a, dqkv_a.shape, (0, 0)), (dqkv_b, dqkv_b.shape, (0, 0))])])
    rs.relay(line)
    rs.side(line)
    head_sums.keep(line)
    gate_sums.half(line)
    gate_sums.quarter(line)
    rs.near(line)
    head_sums.near(line)
    line.wait(rs.other)
    feed_sums.spread(line)
    first, *others = rs.terms()
    line.wait(*others)
    grad_x, late = input_back(tokens_in, grad_middle, [line.hold(first), *others], gain_one)
    line.done(late)
    sums = Summed(line.done(jnp.concatenate([late, early], 0)), ("z", "yl"))
    gate_sums.whole(line)
    gate_sums.spread(line)
    sums.step(line)
    head_sums.half(line)
    head_sums.quarter(line)
    sums.step(line)
    sums.step(line)
    out_rs = Scatter({**out_a, **{p: line.hold(v) for p, v in out_b.items()}})
    feed_sums.last(line)
    gate_sums.last(line)
    head_sums.whole(line)
    head_sums.spread(line)
    sums.step(line)
    wide = jnp.pad(bsum_a + bsum_b, ((0, 0), (0, early.shape[1] - bsum_a.shape[1])))
    sums = Summed(line.done(jnp.concatenate([line.hold(sums.value), wide], 0)), ("c", "yh", "x"))
    sums.step(line)
    out_rs.relay(line)
    out_rs.side(line)
    sums.step(line)
    feed_sums.swap(line)
    grad_up, grad_down = placed(feed_sums.pieces(line), final, (w_up.shape[1], w_down.shape[0]), (False, True))
    line.done(grad_up)
    gate_sums.swap(line)
    grad_gate, grad_out = placed(gate_sums.pieces(line), final, (DV, DV), (False, True))
    line.done(grad_gate)
    sums.step(line)
    head_sums.last(line)
    out_rs.near(line)
    sums.step(line)
    head_sums.swap(line)
    sums.step(line)
    grad_query, grad_key, grad_value = placed(head_sums.pieces(line), final, (DK, DK, DV), (False, False, False))
    line.done(grad_query)
    sums = sums.value
    b_up_sum = sums[5, : bsum_a.shape[1]]
    result = middle + plus(*out_rs.terms()) + b_down
    return (
        result.astype(BF),
        grad_x,
        sums[0],
        sums[1],
        grad_query,
        grad_key,
        grad_value,
        grad_gate,
        grad_out,
        sums[2],
        sums[3],
        grad_up,
        b_up_sum,
        grad_down,
        sums[4],
    )


def solution(mesh):
    split = Mesh(mesh.devices.reshape(4, 2, 2, 2, 4), AXES)
    rows = P(AXES, None)
    cols = P(None, MP)
    mp_rows = P(MP, None)
    return jax.shard_map(
        local,
        mesh=split,
        in_specs=(
            rows, rows, P(DP, None), P(), P(), cols, cols, cols, cols, mp_rows, P(), P(), cols, P(MP), mp_rows, P(),
        ),
        out_specs=(
            rows, rows, P(), P(), cols, cols, cols, cols, mp_rows, P(), P(), cols, P(MP), mp_rows, P(),
        ),
        check_vma=False,
    )
```

time: 1050 us -> 439 us (0.42)
  blocking collectives: 299 us -> 0 us
  waiting for transfers between devices: 444 us -> 188 us
  matrix products: 145 us -> 0 us
  Pallas kernels: 0 us -> 111 us
  starting transfers between devices: 4.93 us -> 97.8 us
  other arithmetic: 89.1 us -> 2.12 us
  between operations: 14.9 us -> 2.31 us
    psum x2 -> x0, blocking collectives: 299 us -> none  [the longest x1 179 us: local(): lax.psum((grad_ln1_gain, grad_ln1_bias, grad_ln2_gain, grad_ln2_bias, gra...]
    reduce_scatter x3 -> x0, waiting for transfers between devices: 228 us -> none  [the longest x1 91.6 us: local(): lax.psum_scatter(jnp.dot(gated, w_out, preferred_element_type=jnp.float32...]
    all_gather x5 -> x0, waiting for transfers between devices: 215 us -> none  [the longest x2 72.9 us: stacked_from(): pieces = lax.all_gather(pieces, axes[k], axis=0, tiled=True)]
    ppermute x0 -> x93, waiting for transfers between devices: none -> 188 us  [the longest x66 91.6 us: shifted(): lax.ppermute(value, axis, [((i + step) % size, i) for i in range(size)])]
    dot_general x31 -> x0, matrix products: 145 us -> none  [the longest x7 57.4 us: contract_cols(): lax.dot_general(left_side, right_side, (((1,), (1,)), ((), ())), preferre...]
    pallas_call x0 -> x59, Pallas kernels: none -> 111 us  [the longest x50 65.8 us: simple(): pl.pallas_call(body, in_specs=in_specs, out_specs=[pl.BlockSpec(memory_sp...]
    ppermute x0 -> x93, starting transfers between devices: none -> 97.8 us  [the longest x66 78.5 us: shifted(): lax.ppermute(value, axis, [((i + step) % size, i) for i in range(size)])]
    convert_element_type x16 -> x1, other arithmetic: 38.7 us -> 1.19 us  [local(): result.astype(BF)]
  transfers between devices with their start and end apart: 10 -> 93, of which waited for: 8 -> 46; matrix products, arithmetic and copies ran while one was open for 5% -> 1% of each run, Pallas kernels for 0% -> 20%
where the time goes in v1:
time: 439 us; the launch traced here: 432 us
  waiting for transfers between devices  188 us (43%)
  Pallas kernels  111 us (25%)
  starting transfers between devices  97.8 us (22%)
  local copies, waits for them, and re-layouts  31 us (7%)
    ppermute x66, waiting for transfers between devices, shifted(): lax.ppermute(value, axis, [((i + step) % size, i) for i in range(size)])  91.6 us
    ppermute x66, starting transfers between devices, shifted(): lax.ppermute(value, axis, [((i + step) % size, i) for i in range(size)])  78.5 us
    ppermute x20, waiting for transfers between devices, by_sides(): return lax.ppermute(value, names, pairs)  71.4 us
    pallas_call x50, Pallas kernels, simple(): pl.pallas_call(body, in_specs=in_specs, out_specs=[pl.BlockSpec(memory_sp...  65.8 us
    unnamed x188, local copies, waits for them, and re-layouts  27.2 us
    pallas_call x6, Pallas kernels, weight_parts(): pl.pallas_call(functools.partial(weight_kernel, counts=[len(lefts) for le...  25.6 us
    ppermute x7, waiting for transfers between devices, step(): self.come = lax.ppermute(self.value, axis, pairs)  25 us
    pallas_call x3, Pallas kernels, placed(): pl.pallas_call(functools.partial(place_kernel, columns=columns, turned=tu...  19.6 us
  transfers between devices with their start and end apart: 93, of which 46 were waited for; matrix products, arithmetic and copies ran while one was open for 1% of the time, Pallas kernels for 20%

profile of v1, /device:TPU:0, one launch (start us, length us, event | category | flops | bytes accessed | tf_op | source)
XLA Modules:
  0.0 432.2 jit_solution(10232327591683866698)
XLA Ops:
  12.1 6.8 %collective-permute-done.first.b1 = bf16[128,2048]{1,0:T(8,128)(2,1)S(1)} collective-permute-done((bf16[128,2048]{1,0:T(8,128)(2,1)S(1)}, bf16[128,2048]{1,0:T(8,128)(2,1)S(1)}, u32[]{:S(2)}, u32[]{:S(2)}) %collective-permute-start) | collective-permute-done | bytes 524320 | tf_op jit(solution)/shard_map/ppermute | solution.py:55
  26.3 9.9 %collective-permute-done.3.b0 = bf16[128,2048]{1,0:T(8,128)(2,1)} collective-permute-done((bf16[128,2048]{1,0:T(8,128)(2,1)S(1)}, bf16[128,2048]{1,0:T(8,128)(2,1)}, u32[]{:S(2)}, u32[]{:S(2)}) %collective-permute-start.3) | collective-permute-done | bytes 524320 | tf_op jit(solution)/shard_map/ppermute | solution.py:69
  40.0 6.5 %heads.2 = (bf16[512,2048]{1,0:T(8,128)(2,1)S(1)}, bf16[512,256]{1,0:T(8,128)(2,1)S(1)}, bf16[512,256]{1,0:T(8,128)(2,1)S(1)}, bf16[512,512]{1,0:T(8,128)(2,1)S(1)}, f32[512,512]{1,0:T(8,128)S(1)}) custom-call(s32[10]{0:T(128)S(1)} %stack.77.marks, bf16[128,2048]{1,0:T(8,128)(2,1)S(1)} %norm.1.b0, bf16[128,2048]{1,0:T(8,128)(2,1)S(1)} %collective-permute-done.first.b1, ...), custom_call_target="tpu_custom_call" | custom-call | tf_op jit(solution)/shard_map/heads/pallas_call | solution.py:191
  50.9 7.2 %heads.3 = (bf16[512,2048]{1,0:T(8,128)(2,1)S(1)}, bf16[512,256]{1,0:T(8,128)(2,1)S(1)}, bf16[512,256]{1,0:T(8,128)(2,1)S(1)}, bf16[512,512]{1,0:T(8,128)(2,1)S(1)}, f32[512,512]{1,0:T(8,128)S(1)}) custom-call(s32[10]{0:T(128)S(1)} %stack.77.marks, bf16[128,2048]{1,0:T(8,128)(2,1)} %collective-permute-done.3.b0, ...), custom_call_target="tpu_custom_call" | custom-call | tf_op jit(solution)/shard_map/heads/pallas_call | solution.py:191
  83.9 7.8 %collective-permute-done.15.passed = bf16[128,2048]{1,0:T(8,128)(2,1)S(1)} collective-permute-done((bf16[128,2048]{1,0:T(8,128)(2,1)S(1)}, bf16[128,2048]{1,0:T(8,128)(2,1)S(1)}, u32[]{:S(2)}, u32[]{:S(2)}) %collective-permute-start.15) | collective-permute-done | bytes 524320 | tf_op jit(solution)/shard_map/ppermute | solution.py:69
  123.7 7.1 %collective-permute-done.24.b0 = bf16[128,2048]{1,0:T(8,128)(2,1)S(1)} collective-permute-done((bf16[128,2048]{1,0:T(8,128)(2,1)S(1)}, bf16[128,2048]{1,0:T(8,128)(2,1)S(1)}, u32[]{:S(2)}, u32[]{:S(2)}) %collective-permute-start.24) | collective-permute-done | bytes 524320 | tf_op jit(solution)/shard_map/ppermute | solution.py:69
  169.6 10.2 %collective-permute-done.31.passed = bf16[128,2048]{1,0:T(8,128)(2,1)S(1)} collective-permute-done((bf16[128,2048]{1,0:T(8,128)(2,1)S(1)}, bf16[128,2048]{1,0:T(8,128)(2,1)S(1)}, u32[]{:S(2)}, u32[]{:S(2)}) %collective-permute-start.31) | collective-permute-done | bytes 524320 | tf_op jit(solution)/shard_map/ppermute | solution.py:69
  183.4 4.6 %weight_parts.7 = (bf16[256,1024]{1,0:T(8,128)(2,1)S(1)}, bf16[512,1024]{1,0:T(8,128)(2,1)S(1)}, bf16[256,1024]{1,0:T(8,128)(2,1)S(1)}) custom-call(s32[8]{0:T(128)S(1)} %copy-done.83, bf16[512,2048]{1,0:T(8,128)(2,1)S(1)} %copy-done.17, bf16[512,2048]{1,0:T(8,128)(2,1)S(1)} %copy-done.19, bf16[512,512]{1,0:T(8,128)(2,1)S(1)} %copy-done.43, ...), custom_call_target="tpu_custom_call" | custom-call | tf_op jit(solution)/shard_map/weight_parts/pallas_call | solution.py:641
  189.5 4.4 %collective-permute-done.34.up = bf16[128,2048]{1,0:T(8,128)(2,1)S(1)} collective-permute-done((bf16[128,2048]{1,0:T(8,128)(2,1)S(1)}, bf16[128,2048]{1,0:T(8,128)(2,1)S(1)}, u32[]{:S(2)}, u32[]{:S(2)}) %collective-permute-start.34) | collective-permute-done | bytes 524320 | tf_op jit(solution)/shard_map/ppermute | solution.py:55
  202.0 7.3 %collective-permute-done.36.first.b1 = bf16[128,2048]{1,0:T(8,128)(2,1)S(1)} collective-permute-done((bf16[128,2048]{1,0:T(8,128)(2,1)S(1)}, bf16[128,2048]{1,0:T(8,128)(2,1)S(1)}, u32[]{:S(2)}, u32[]{:S(2)}) %collective-permute-start.36) | collective-permute-done | bytes 524320 | tf_op jit(solution)/shard_map/ppermute | solution.py:55
  213.5 9.0 %collective-permute-done.40.b0 = bf16[128,2048]{1,0:T(8,128)(2,1)S(1)} collective-permute-done((bf16[128,2048]{1,0:T(8,128)(2,1)S(1)}, bf16[128,2048]{1,0:T(8,128)(2,1)S(1)}, u32[]{:S(2)}, u32[]{:S(2)}) %collective-permute-start.40) | collective-permute-done | bytes 524320 | tf_op jit(solution)/shard_map/ppermute | solution.py:69
  228.1 10.8 %collective-permute-done.43.b1 = bf16[128,2048]{1,0:T(8,128)(2,1)S(1)} collective-permute-done((bf16[128,2048]{1,0:T(8,128)(2,1)S(1)}, bf16[128,2048]{1,0:T(8,128)(2,1)S(1)}, u32[]{:S(2)}, u32[]{:S(2)}) %collective-permute-start.43) | collective-permute-done | bytes 524320 | tf_op jit(solution)/shard_map/ppermute | solution.py:55
  251.5 7.2 %retain_back.1 = (bf16[512,1024]{1,0:T(8,128)(2,1)S(1)}, bf16[512,1024]{1,0:T(8,128)(2,1)S(1)}) custom-call(s32[10]{0:T(128)S(1)} %copy-done.85, f32[1]{0:T(128)} %bitcast.11.decay, bf16[512,256]{1,0:T(8,128)(2,1)S(1)} %copy-done.58, bf16[512,256]{1,0:T(8,128)(2,1)S(1)} %copy-done.60, bf16[512,256]{1,0:T(8,128)(2,1)S(1)} %get-tuple-element.199.kr_a, ...), custom_call_target="tpu_custom_call" | custom-call | tf_op jit(solution)/shard_map/retain_back/pallas_call | solution.py:191
  258.8 4.6 %weight_parts.9 = (bf16[256,1024]{1,0:T(8,128)(2,1)S(1)}, bf16[512,1024]{1,0:T(8,128)(2,1)S(1)}, bf16[256,1024]{1,0:T(8,128)(2,1)S(1)}) custom-call(s32[8]{0:T(128)S(1)} %copy-done.83, bf16[512,2048]{1,0:T(8,128)(2,1)S(1)} %copy-done.6, bf16[512,2048]{1,0:T(8,128)(2,1)S(1)} %copy-done.8, bf16[512,512]{1,0:T(8,128)(2,1)S(1)} %get-tuple-element.285.refs_2_.dgate, ...), custom_call_target="tpu_custom_call" | custom-call | tf_op jit(solution)/shard_map/weight_parts/pallas_call | solution.py:641
  282.8 10.0 %collective-permute-done.49.refs_1_ = bf16[128,2048]{1,0:T(8,128)(2,1)S(1)} collective-permute-done((bf16[128,2048]{1,0:T(8,128)(2,1)S(1)}, bf16[128,2048]{1,0:T(8,128)(2,1)S(1)}, u32[]{:S(2)}, u32[]{:S(2)}) %collective-permute-start.49) | collective-permute-done | bytes 524320 | tf_op jit(solution)/shard_map/ppermute | solution.py:55
  305.1 5.4 %collective-permute-done.55.passed = bf16[128,2048]{1,0:T(8,128)(2,1)S(1)} collective-permute-done((bf16[128,2048]{1,0:T(8,128)(2,1)S(1)}, bf16[128,2048]{1,0:T(8,128)(2,1)S(1)}, u32[]{:S(2)}, u32[]{:S(2)}) %collective-permute-start.55) | collective-permute-done | bytes 524320 | tf_op jit(solution)/shard_map/ppermute | solution.py:69
  318.8 6.9 %collective-permute-done.59.up = bf16[128,2048]{1,0:T(8,128)(2,1)S(1)} collective-permute-done((bf16[128,2048]{1,0:T(8,128)(2,1)S(1)}, bf16[128,2048]{1,0:T(8,128)(2,1)S(1)}, u32[]{:S(2)}, u32[]{:S(2)}) %collective-permute-start.59) | collective-permute-done | bytes 524320 | tf_op jit(solution)/shard_map/ppermute | solution.py:55
  337.2 4.3 collective-permute-done.65
  350.3 9.9 %collective-permute-done.67.both.refs_1_ = bf16[512,1024]{1,0:T(8,128)(2,1)S(1)} collective-permute-done((bf16[512,1024]{1,0:T(8,128)(2,1)S(1)}, bf16[512,1024]{1,0:T(8,128)(2,1)S(1)}, u32[]{:S(2)}, u32[]{:S(2)}) %collective-permute-start.67) | collective-permute-done | bytes 1048608 | tf_op jit(solution)/shard_map/ppermute | solution.py:69
  366.8 10.3 %collective-permute-done.71 = f32[5,2048]{1,0:T(8,128)S(1)} collective-permute-done((f32[5,2048]{1,0:T(8,128)S(1)}, f32[5,2048]{1,0:T(8,128)S(1)}, u32[]{:S(2)}, u32[]{:S(2)}) %collective-permute-start.71) | collective-permute-done | bytes 40992 | tf_op jit(solution)/shard_map/ppermute | solution.py:162
  383.1 8.1 %placed.3 = (f32[2048,512]{1,0:T(8,128)}, f32[512,2048]{1,0:T(8,128)}) custom-call(s32[8]{0:T(128)S(1)} %stack.89.places, bf16[512,1024]{1,0:T(8,128)(2,1)S(1)} %both.3.refs_0_, bf16[512,1024]{1,0:T(8,128)(2,1)} %collective-permute-done.68.both.refs_1_, bf16[512,1024]{1,0:T(8,128)(2,1)} %collective-permute-done.79.refs_2_, ...), custom_call_target="tpu_custom_call" | custom-call | tf_op jit(solution)/shard_map/placed/pallas_call | solution.py:766
  395.0 6.4 %placed.4 = (f32[2048,512]{1,0:T(8,128)}, f32[512,2048]{1,0:T(8,128)}) custom-call(s32[8]{0:T(128)S(1)} %stack.89.places, bf16[512,1024]{1,0:T(8,128)(2,1)S(1)} %both.4.refs_0_, bf16[512,1024]{1,0:T(8,128)(2,1)S(1)} %copy-done.28, bf16[512,1024]{1,0:T(8,128)(2,1)S(1)} %collective-permute-done.82.refs_2_, bf16[256,1024]{1,0:T(8,128)(2,1)} %collective-permute-done.81.refs_3_, ...), custom_call_target="tpu_custom_call" | custom-call | tf_op jit(solution)/shard_map/placed/pallas_call | solution.py:766
  401.4 6.4 %collective-permute-done.76.both.refs_1_ = bf16[512,1024]{1,0:T(8,128)(2,1)S(1)} collective-permute-done((bf16[512,1024]{1,0:T(8,128)(2,1)S(1)}, bf16[512,1024]{1,0:T(8,128)(2,1)S(1)}, u32[]{:S(2)}, u32[]{:S(2)}) %collective-permute-start.76) | collective-permute-done | bytes 1048608 | tf_op jit(solution)/shard_map/ppermute | solution.py:69
  426.9 5.1 %placed.5 = (f32[2048,256]{1,0:T(8,128)}, f32[2048,256]{1,0:T(8,128)}, f32[2048,512]{1,0:T(8,128)}) custom-call(s32[8]{0:T(128)S(1)} %stack.89.places, bf16[512,1024]{1,0:T(8,128)(2,1)S(1)} %both.5.refs_0_, bf16[512,1024]{1,0:T(8,128)(2,1)S(1)} %collective-permute-done.76.both.refs_1_, bf16[512,1024]{1,0:T(8,128)(2,1)S(1)} %collective-permute-done.91.refs_2_, ...), custom_call_target="tpu_custom_call" | custom-call | tf_op jit(solution)/shard_map/placed/pallas_call | solution.py:766
  (427 shorter events, 254.0 us)
Async XLA Ops:
  24.3 23.5 %collective-permute-start.5 = (bf16[128,2048]{1,0:T(8,128)(2,1)S(1)}, bf16[128,2048]{1,0:T(8,128)(2,1)}, u32[]{:S(2)}, u32[]{:S(2)}) collective-permute-start(bf16[128,2048]{1,0:T(8,128)(2,1)S(1)} %collective-permute-done.1.b3), channel_id=1, source_target_pairs={{1,0},{2,1},{3,2},{0,3},{5,4},{6,5},{7,6},{4,7},{9,8},{10,9},{11,1... | collective-permute-start | bytes 1572872 | tf_op jit(solution)/shard_map/ppermute | solution.py:55
  24.4 26.3 %collective-permute-start.6 = (bf16[128,2048]{1,0:T(8,128)(2,1)S(1)}, bf16[128,2048]{1,0:T(8,128)(2,1)}, u32[]{:S(2)}, u32[]{:S(2)}) collective-permute-start(bf16[128,2048]{1,0:T(8,128)(2,1)S(1)} %collective-permute-done.1.b3), channel_id=1, source_target_pairs={{3,0},{0,1},{1,2},{2,3},{7,4},{4,5},{5,6},{6,7},{11,8},{8,9},{9,10... | collective-permute-start | bytes 1572872 | tf_op jit(solution)/shard_map/ppermute | solution.py:55
  37.9 27.7 %collective-permute-start.8 = (bf16[128,2048]{1,0:T(8,128)(2,1)}, bf16[128,2048]{1,0:T(8,128)(2,1)S(1)}, u32[]{:S(2)}, u32[]{:S(2)}) collective-permute-start(bf16[128,2048]{1,0:T(8,128)(2,1)} %cot.1), channel_id=1, source_target_pairs={{1,0},{2,1},{3,2},{0,3},{5,4},{6,5},{7,6},{4,7},{9,8},{10,9},{11,1... | collective-permute-start | bytes 1572872 | tf_op jit(solution)/shard_map/ppermute | solution.py:55
  39.6 26.0 %collective-permute-start.9 = (bf16[128,2048]{1,0:T(8,128)(2,1)}, bf16[128,2048]{1,0:T(8,128)(2,1)S(1)}, u32[]{:S(2)}, u32[]{:S(2)}) collective-permute-start(bf16[128,2048]{1,0:T(8,128)(2,1)} %cot.1), channel_id=1, source_target_pairs={{3,0},{0,1},{1,2},{2,3},{7,4},{4,5},{5,6},{6,7},{11,8},{8,9},{9,10... | collective-permute-start | bytes 1572872 | tf_op jit(solution)/shard_map/ppermute | solution.py:55
  47.8 21.1 %collective-permute-start.10 = (bf16[128,2048]{1,0:T(8,128)(2,1)}, bf16[128,2048]{1,0:T(8,128)(2,1)S(1)}, u32[]{:S(2)}, u32[]{:S(2)}) collective-permute-start(bf16[128,2048]{1,0:T(8,128)(2,1)} %collective-permute-done.4.b3), channel_id=1, source_target_pairs={{1,0},{2,1},{3,2},{0,3},{5,4},{6,5},{7,6},{4,7},{9,8},{10,9},{11,1... | collective-permute-start | bytes 1572872 | tf_op jit(solution)/shard_map/ppermute | solution.py:55
  50.7 18.2 %collective-permute-start.11 = (bf16[128,2048]{1,0:T(8,128)(2,1)}, bf16[128,2048]{1,0:T(8,128)(2,1)S(1)}, u32[]{:S(2)}, u32[]{:S(2)}) collective-permute-start(bf16[128,2048]{1,0:T(8,128)(2,1)} %collective-permute-done.4.b3), channel_id=1, source_target_pairs={{3,0},{0,1},{1,2},{2,3},{7,4},{4,5},{5,6},{6,7},{11,8},{8,9},{9,10... | collective-permute-start | bytes 1572872 | tf_op jit(solution)/shard_map/ppermute | solution.py:55
  75.7 16.1 %collective-permute-start.15 = (bf16[128,2048]{1,0:T(8,128)(2,1)S(1)}, bf16[128,2048]{1,0:T(8,128)(2,1)S(1)}, u32[]{:S(2)}, u32[]{:S(2)}) collective-permute-start(bf16[128,2048]{1,0:T(8,128)(2,1)S(1)} %added.11), channel_id=1, source_target_pairs={{3,0},{0,1},{1,2},{2,3},{9,8},{10,9},{11,10},{8,11},{7,4},{4,5},{5... | collective-permute-start | bytes 1572872 | tf_op jit(solution)/shard_map/ppermute | solution.py:69
  78.0 22.4 %collective-permute-start.17 = (bf16[128,2048]{1,0:T(8,128)(2,1)S(1)}, bf16[128,2048]{1,0:T(8,128)(2,1)S(1)}, u32[]{:S(2)}, u32[]{:S(2)}) collective-permute-start(bf16[128,2048]{1,0:T(8,128)(2,1)S(1)} %added.12), channel_id=1, source_target_pairs={{4,0},{0,4},{5,1},{1,5},{6,2},{2,6},{7,3},{3,7},{12,8},{8,12},{13,... | collective-permute-start | bytes 1572872 | tf_op jit(solution)/shard_map/ppermute | solution.py:55
  80.2 19.0 %collective-permute-start.16 = (bf16[128,2048]{1,0:T(8,128)(2,1)S(1)}, bf16[128,2048]{1,0:T(8,128)(2,1)S(1)}, u32[]{:S(2)}, u32[]{:S(2)}) collective-permute-start(bf16[128,2048]{1,0:T(8,128)(2,1)S(1)} %chosen.5), channel_id=1, source_target_pairs={{1,0},{2,1},{3,2},{0,3},{11,8},{8,9},{9,10},{10,11},{5,4},{6,5},{7... | collective-permute-start | bytes 1572872 | tf_op jit(solution)/shard_map/ppermute | solution.py:69
  121.6 18.2 %collective-permute-start.25 = (bf16[128,2048]{1,0:T(8,128)(2,1)S(1)}, bf16[128,2048]{1,0:T(8,128)(2,1)S(1)}, u32[]{:S(2)}, u32[]{:S(2)}) collective-permute-start(bf16[128,2048]{1,0:T(8,128)(2,1)S(1)} %collective-permute-done.22.b3), channel_id=1, source_target_pairs={{1,0},{2,1},{3,2},{0,3},{5,4},{6,5},{7,6},{4,7},{9,8},{10,9},{11,1... | collective-permute-start | bytes 1572872 | tf_op jit(solution)/shard_map/ppermute | solution.py:55
  121.7 18.2 %collective-permute-start.26 = (bf16[128,2048]{1,0:T(8,128)(2,1)S(1)}, bf16[128,2048]{1,0:T(8,128)(2,1)S(1)}, u32[]{:S(2)}, u32[]{:S(2)}) collective-permute-start(bf16[128,2048]{1,0:T(8,128)(2,1)S(1)} %collective-permute-done.22.b3), channel_id=1, source_target_pairs={{3,0},{0,1},{1,2},{2,3},{7,4},{4,5},{5,6},{6,7},{11,8},{8,9},{9,10... | collective-permute-start | bytes 1572872 | tf_op jit(solution)/shard_map/ppermute | solution.py:55
  169.4 20.1 %collective-permute-start.33 = (bf16[128,2048]{1,0:T(8,128)(2,1)S(1)}, bf16[128,2048]{1,0:T(8,128)(2,1)S(1)}, u32[]{:S(2)}, u32[]{:S(2)}) collective-permute-start(bf16[128,2048]{1,0:T(8,128)(2,1)S(1)} %added.14), channel_id=1, source_target_pairs={{4,0},{0,4},{5,1},{1,5},{6,2},{2,6},{7,3},{3,7},{12,8},{8,12},{13,... | collective-permute-start | bytes 1572872 | tf_op jit(solution)/shard_map/ppermute | solution.py:55
  200.5 23.8 %collective-permute-start.41 = (bf16[512,1024]{1,0:T(8,128)(2,1)S(1)}, bf16[512,1024]{1,0:T(8,128)(2,1)S(1)}, u32[]{:S(2)}, u32[]{:S(2)}) collective-permute-start(bf16[512,1024]{1,0:T(8,128)(2,1)S(1)} %near.3), channel_id=1, source_target_pairs={{96,0},{0,32},{32,64},{64,96},{40,8},{72,40},{104,72},{8,104},{97,... | collective-permute-start | bytes 3145736 | tf_op jit(solution)/shard_map/ppermute | solution.py:69
  248.1 17.0 %collective-permute-start.47 = (bf16[256,1024]{1,0:T(8,128)(2,1)S(1)}, bf16[256,1024]{1,0:T(8,128)(2,1)S(1)}, u32[]{:S(2)}, u32[]{:S(2)}) collective-permute-start(bf16[256,1024]{1,0:T(8,128)(2,1)S(1)} %quarter.3.refs_0_), channel_id=1, source_target_pairs={{16,0},{0,16},{17,1},{1,17},{18,2},{2,18},{19,3},{3,19},{20,4},{4,... | collective-permute-start | bytes 1572872 | tf_op jit(solution)/shard_map/ppermute | solution.py:55
  278.1 17.5 %collective-permute-start.52 = (bf16[1024,1024]{1,0:T(8,128)(2,1)S(1)}, bf16[1024,1024]{1,0:T(8,128)(2,1)S(1)}, u32[]{:S(2)}, u32[]{:S(2)}) collective-permute-start(bf16[1024,1024]{1,0:T(8,128)(2,1)S(1)} %weight_parts.10), channel_id=1, source_target_pairs={{8,0},{0,8},{9,1},{1,9},{10,2},{2,10},{11,3},{3,11},{12,4},{4,12},... | collective-permute-start | bytes 6291464 | tf_op jit(solution)/shard_map/ppermute | solution.py:55
  278.2 21.5 %collective-permute-start.53 = (bf16[512,1024]{1,0:T(8,128)(2,1)S(1)}, bf16[512,1024]{1,0:T(8,128)(2,1)S(1)}, u32[]{:S(2)}, u32[]{:S(2)}) collective-permute-start(bf16[512,1024]{1,0:T(8,128)(2,1)S(1)} %near.4), channel_id=1, source_target_pairs={{96,0},{0,32},{32,64},{64,96},{40,8},{72,40},{104,72},{8,104},{97,... | collective-permute-start | bytes 3145736 | tf_op jit(solution)/shard_map/ppermute | solution.py:69
  316.5 16.5 %collective-permute-start.61 = (bf16[512,1024]{1,0:T(8,128)(2,1)S(1)}, bf16[512,1024]{1,0:T(8,128)(2,1)S(1)}, u32[]{:S(2)}, u32[]{:S(2)}) collective-permute-start(bf16[512,1024]{1,0:T(8,128)(2,1)S(1)} %near.5), channel_id=1, source_target_pairs={{96,0},{0,32},{32,64},{64,96},{40,8},{72,40},{104,72},{8,104},{97,... | collective-permute-start | bytes 3145736 | tf_op jit(solution)/shard_map/ppermute | solution.py:69
  333.0 16.1 %collective-permute-start.68 = (bf16[512,1024]{1,0:T(8,128)(2,1)S(1)}, bf16[512,1024]{1,0:T(8,128)(2,1)}, u32[]{:S(2)}, u32[]{:S(2)}) collective-permute-start(bf16[512,1024]{1,0:T(8,128)(2,1)S(1)} %both.3.refs_0_), channel_id=1, source_target_pairs={{96,0},{0,32},{32,64},{64,96},{40,8},{72,40},{104,72},{8,104},{97,... | collective-permute-start | bytes 3145736 | tf_op jit(solution)/shard_map/ppermute | solution.py:69
  333.2 27.0 %collective-permute-start.67 = (bf16[512,1024]{1,0:T(8,128)(2,1)S(1)}, bf16[512,1024]{1,0:T(8,128)(2,1)S(1)}, u32[]{:S(2)}, u32[]{:S(2)}) collective-permute-start(bf16[512,1024]{1,0:T(8,128)(2,1)S(1)} %both.4.refs_0_), channel_id=1, source_target_pairs={{96,0},{0,32},{32,64},{64,96},{40,8},{72,40},{104,72},{8,104},{97,... | collective-permute-start | bytes 3145736 | tf_op jit(solution)/shard_map/ppermute | solution.py:69
  335.8 25.3 %collective-permute-start.69 = (bf16[256,1024]{1,0:T(8,128)(2,1)S(1)}, bf16[256,1024]{1,0:T(8,128)(2,1)S(1)}, u32[]{:S(2)}, u32[]{:S(2)}) collective-permute-start(bf16[256,1024]{1,0:T(8,128)(2,1)S(1)} %quarter.5.refs_0_), channel_id=1, source_target_pairs={{16,0},{0,16},{17,1},{1,17},{18,2},{2,18},{19,3},{3,19},{20,4},{4,... | collective-permute-start | bytes 1572872 | tf_op jit(solution)/shard_map/ppermute | solution.py:55
  361.4 15.9 %collective-permute-start.72 = (bf16[128,2048]{1,0:T(8,128)(2,1)S(1)}, bf16[128,2048]{1,0:T(8,128)(2,1)S(1)}, u32[]{:S(2)}, u32[]{:S(2)}) collective-permute-start(bf16[128,2048]{1,0:T(8,128)(2,1)S(1)} %get-tuple-element.337), channel_id=1, source_target_pairs={{4,0},{0,4},{5,1},{1,5},{6,2},{2,6},{7,3},{3,7},{12,8},{8,12},{13,... | collective-permute-start | bytes 1572872 | tf_op jit(solution)/shard_map/ppermute | solution.py:55
  361.5 16.6 %collective-permute-start.73 = (bf16[128,2048]{1,0:T(8,128)(2,1)S(1)}, bf16[128,2048]{1,0:T(8,128)(2,1)S(1)}, u32[]{:S(2)}, u32[]{:S(2)}) collective-permute-start(bf16[128,2048]{1,0:T(8,128)(2,1)S(1)} %get-tuple-element.340), channel_id=1, source_target_pairs={{3,0},{0,1},{1,2},{2,3},{7,4},{4,5},{5,6},{6,7},{11,8},{8,9},{9,10... | collective-permute-start | bytes 1572872 | tf_op jit(solution)/shard_map/ppermute | solution.py:55
  361.5 16.6 %collective-permute-start.74 = (bf16[128,2048]{1,0:T(8,128)(2,1)S(1)}, bf16[128,2048]{1,0:T(8,128)(2,1)S(1)}, u32[]{:S(2)}, u32[]{:S(2)}) collective-permute-start(bf16[128,2048]{1,0:T(8,128)(2,1)S(1)} %get-tuple-element.342), channel_id=1, source_target_pairs={{1,0},{2,1},{3,2},{0,3},{5,4},{6,5},{7,6},{4,7},{9,8},{10,9},{11,1... | collective-permute-start | bytes 1572872 | tf_op jit(solution)/shard_map/ppermute | solution.py:55
  391.7 16.0 %collective-permute-start.76 = (bf16[512,1024]{1,0:T(8,128)(2,1)S(1)}, bf16[512,1024]{1,0:T(8,128)(2,1)S(1)}, u32[]{:S(2)}, u32[]{:S(2)}) collective-permute-start(bf16[512,1024]{1,0:T(8,128)(2,1)S(1)} %both.5.refs_0_), channel_id=1, source_target_pairs={{96,0},{0,32},{32,64},{64,96},{40,8},{72,40},{104,72},{8,104},{97,... | collective-permute-start | bytes 3145736 | tf_op jit(solution)/shard_map/ppermute | solution.py:69
  (163 other events, 1720.6 us)

commit v2 on v1

--- a/solution.py
+++ b/solution.py
@@ -926,7 +926,6 @@
     rs.near(line)
     head_sums.near(line)
     line.wait(rs.other)
-    feed_sums.spread(line)
     first, *others = rs.terms()
     line.wait(*others)
     grad_x, late = input_back(tokens_in, grad_middle, [line.hold(first), *others], gain_one)
@@ -939,35 +938,38 @@
     head_sums.quarter(line)
     sums.step(line)
     sums.step(line)
-    out_rs = Scatter({**out_a, **{p: line.hold(v) for p, v in out_b.items()}})
-    feed_sums.last(line)
     gate_sums.last(line)
+    feed_sums.spread(line)
     head_sums.whole(line)
     head_sums.spread(line)
     sums.step(line)
     wide = jnp.pad(bsum_a + bsum_b, ((0, 0), (0, early.shape[1] - bsum_a.shape[1])))
     sums = Summed(line.done(jnp.concatenate([line.hold(sums.value), wide], 0)), ("c", "yh", "x"))
     sums.step(line)
+    out_rs = Scatter({**out_a, **{p: line.hold(v) for p, v in out_b.items()}})
+    gate_sums.swap(line)
+    sums.step(line)
+    feed_sums.last(line)
+    gate_pieces = [in_hbm(p) for p in gate_sums.pieces(line)]
+    grad_gate, grad_out = placed(gate_pieces, final, (DV, DV), (False, True))
+    line.done(grad_gate)
+    head_sums.last(line)
     out_rs.relay(line)
     out_rs.side(line)
-    sums.step(line)
     feed_sums.swap(line)
     grad_up, grad_down = placed(feed_sums.pieces(line), final, (w_up.shape[1], w_down.shape[0]), (False, True))
     line.done(grad_up)
-    gate_sums.swap(line)
-    grad_gate, grad_out = placed(gate_sums.pieces(line), final, (DV, DV), (False, True))
-    line.done(grad_gate)
-    sums.step(line)
-    head_sums.last(line)
     out_rs.near(line)
     sums.step(line)
     head_sums.swap(line)
     sums.step(line)
     grad_query, grad_key, grad_value = placed(head_sums.pieces(line), final, (DK, DK, DV), (False, False, False))
-    line.done(grad_query)
+    sums.step(line)
+    line.wait(grad_query)
     sums = sums.value
     b_up_sum = sums[5, : bsum_a.shape[1]]
-    result = middle + plus(*out_rs.terms()) + b_down
+    first, *others = out_rs.terms()
+    result = middle + plus(line.hold(first), *others) + b_down
     return (
         result.astype(BF),
         grad_x,

time: 439 us -> 432 us (0.984)
  starting transfers between devices: 97.8 us -> 92.4 us
    ppermute x7, waiting for transfers between devices: 25 us -> 19.2 us  [step(): self.come = lax.ppermute(self.value, axis, pairs)]
    unnamed x188 -> x198, local copies, waits for them, and re-layouts: 27.2 us -> 26.6 us
  transfers between devices with their start and end apart: 93 -> 93, of which waited for: 46 -> 49; matrix products, arithmetic and copies ran while one was open for 1% -> 1% of each run, Pallas kernels for 20% -> 22%
where the time goes in v2:
time: 432 us; the launch traced here: 426 us
  waiting for transfers between devices  185 us (43%)
  Pallas kernels  113 us (26%)
  starting transfers between devices  92.4 us (21%)
  local copies, waits for them, and re-layouts  30.4 us (7%)
    ppermute x66, waiting for transfers between devices, shifted(): lax.ppermute(value, axis, [((i + step) % size, i) for i in range(size)])  93.8 us
    ppermute x66, starting transfers between devices, shifted(): lax.ppermute(value, axis, [((i + step) % size, i) for i in range(size)])  75.7 us
    ppermute x20, waiting for transfers between devices, by_sides(): return lax.ppermute(value, names, pairs)  72.5 us
    pallas_call x50, Pallas kernels, simple(): pl.pallas_call(body, in_specs=in_specs, out_specs=[pl.BlockSpec(memory_sp...  67.8 us
    unnamed x198, local copies, waits for them, and re-layouts  26.6 us
    pallas_call x6, Pallas kernels, weight_parts(): pl.pallas_call(functools.partial(weight_kernel, counts=[len(lefts) for le...  25.6 us
    pallas_call x3, Pallas kernels, placed(): pl.pallas_call(functools.partial(place_kernel, columns=columns, turned=tu...  19.8 us
    ppermute x7, waiting for transfers between devices, step(): self.come = lax.ppermute(self.value, axis, pairs)  19.2 us
  transfers between devices with their start and end apart: 93, of which 49 were waited for; matrix products, arithmetic and copies ran while one was open for 1% of the time, Pallas kernels for 22%

profile of v2, /device:TPU:0, one launch (start us, length us, event | category | flops | bytes accessed | tf_op | source)
XLA Modules:
  0.0 426.0 jit_solution(2404740932033170091)
XLA Ops:
  12.1 6.8 %collective-permute-done.first.b1 = bf16[128,2048]{1,0:T(8,128)(2,1)S(1)} collective-permute-done((bf16[128,2048]{1,0:T(8,128)(2,1)S(1)}, bf16[128,2048]{1,0:T(8,128)(2,1)S(1)}, u32[]{:S(2)}, u32[]{:S(2)}) %collective-permute-start) | collective-permute-done | bytes 524320 | tf_op jit(solution)/shard_map/ppermute | solution.py:55
  26.3 9.9 %collective-permute-done.3.b0 = bf16[128,2048]{1,0:T(8,128)(2,1)} collective-permute-done((bf16[128,2048]{1,0:T(8,128)(2,1)S(1)}, bf16[128,2048]{1,0:T(8,128)(2,1)}, u32[]{:S(2)}, u32[]{:S(2)}) %collective-permute-start.3) | collective-permute-done | bytes 524320 | tf_op jit(solution)/shard_map/ppermute | solution.py:69
  40.0 6.5 %heads.2 = (bf16[512,2048]{1,0:T(8,128)(2,1)S(1)}, bf16[512,256]{1,0:T(8,128)(2,1)S(1)}, bf16[512,256]{1,0:T(8,128)(2,1)S(1)}, bf16[512,512]{1,0:T(8,128)(2,1)S(1)}, f32[512,512]{1,0:T(8,128)S(1)}) custom-call(s32[10]{0:T(128)S(1)} %stack.77.marks, bf16[128,2048]{1,0:T(8,128)(2,1)S(1)} %norm.1.b0, bf16[128,2048]{1,0:T(8,128)(2,1)S(1)} %collective-permute-done.first.b1, ...), custom_call_target="tpu_custom_call" | custom-call | tf_op jit(solution)/shard_map/heads/pallas_call | solution.py:191
  50.9 7.2 %heads.3 = (bf16[512,2048]{1,0:T(8,128)(2,1)S(1)}, bf16[512,256]{1,0:T(8,128)(2,1)S(1)}, bf16[512,256]{1,0:T(8,128)(2,1)S(1)}, bf16[512,512]{1,0:T(8,128)(2,1)S(1)}, f32[512,512]{1,0:T(8,128)S(1)}) custom-call(s32[10]{0:T(128)S(1)} %stack.77.marks, bf16[128,2048]{1,0:T(8,128)(2,1)} %collective-permute-done.3.b0, ...), custom_call_target="tpu_custom_call" | custom-call | tf_op jit(solution)/shard_map/heads/pallas_call | solution.py:191
  83.9 7.8 %collective-permute-done.15.passed = bf16[128,2048]{1,0:T(8,128)(2,1)S(1)} collective-permute-done((bf16[128,2048]{1,0:T(8,128)(2,1)S(1)}, bf16[128,2048]{1,0:T(8,128)(2,1)S(1)}, u32[]{:S(2)}, u32[]{:S(2)}) %collective-permute-start.15) | collective-permute-done | bytes 524320 | tf_op jit(solution)/shard_map/ppermute | solution.py:69
  123.7 7.1 %collective-permute-done.24.b0 = bf16[128,2048]{1,0:T(8,128)(2,1)S(1)} collective-permute-done((bf16[128,2048]{1,0:T(8,128)(2,1)S(1)}, bf16[128,2048]{1,0:T(8,128)(2,1)S(1)}, u32[]{:S(2)}, u32[]{:S(2)}) %collective-permute-start.24) | collective-permute-done | bytes 524320 | tf_op jit(solution)/shard_map/ppermute | solution.py:69
  170.2 10.2 %collective-permute-done.31.passed = bf16[128,2048]{1,0:T(8,128)(2,1)S(1)} collective-permute-done((bf16[128,2048]{1,0:T(8,128)(2,1)S(1)}, bf16[128,2048]{1,0:T(8,128)(2,1)S(1)}, u32[]{:S(2)}, u32[]{:S(2)}) %collective-permute-start.31) | collective-permute-done | bytes 524320 | tf_op jit(solution)/shard_map/ppermute | solution.py:69
  184.0 4.5 %weight_parts.7 = (bf16[256,1024]{1,0:T(8,128)(2,1)S(1)}, bf16[512,1024]{1,0:T(8,128)(2,1)S(1)}, bf16[256,1024]{1,0:T(8,128)(2,1)S(1)}) custom-call(s32[8]{0:T(128)S(1)} %copy-done.85, bf16[512,2048]{1,0:T(8,128)(2,1)S(1)} %copy-done.17, bf16[512,2048]{1,0:T(8,128)(2,1)S(1)} %copy-done.19, bf16[512,512]{1,0:T(8,128)(2,1)S(1)} %copy-done.45, ...), custom_call_target="tpu_custom_call" | custom-call | tf_op jit(solution)/shard_map/weight_parts/pallas_call | solution.py:641
  202.0 7.4 %collective-permute-done.36.first.b1 = bf16[128,2048]{1,0:T(8,128)(2,1)S(1)} collective-permute-done((bf16[128,2048]{1,0:T(8,128)(2,1)S(1)}, bf16[128,2048]{1,0:T(8,128)(2,1)S(1)}, u32[]{:S(2)}, u32[]{:S(2)}) %collective-permute-start.36) | collective-permute-done | bytes 524320 | tf_op jit(solution)/shard_map/ppermute | solution.py:55
  213.4 9.1 %collective-permute-done.40.b0 = bf16[128,2048]{1,0:T(8,128)(2,1)S(1)} collective-permute-done((bf16[128,2048]{1,0:T(8,128)(2,1)S(1)}, bf16[128,2048]{1,0:T(8,128)(2,1)S(1)}, u32[]{:S(2)}, u32[]{:S(2)}) %collective-permute-start.40) | collective-permute-done | bytes 524320 | tf_op jit(solution)/shard_map/ppermute | solution.py:69
  228.1 10.8 %collective-permute-done.43.b1 = bf16[128,2048]{1,0:T(8,128)(2,1)S(1)} collective-permute-done((bf16[128,2048]{1,0:T(8,128)(2,1)S(1)}, bf16[128,2048]{1,0:T(8,128)(2,1)S(1)}, u32[]{:S(2)}, u32[]{:S(2)}) %collective-permute-start.43) | collective-permute-done | bytes 524320 | tf_op jit(solution)/shard_map/ppermute | solution.py:55
  243.6 4.2 weight_parts.8
  251.5 7.2 %retain_back.1 = (bf16[512,1024]{1,0:T(8,128)(2,1)S(1)}, bf16[512,1024]{1,0:T(8,128)(2,1)S(1)}) custom-call(s32[10]{0:T(128)S(1)} %copy-done.87, f32[1]{0:T(128)} %bitcast.11.decay, bf16[512,256]{1,0:T(8,128)(2,1)S(1)} %copy-done.60, bf16[512,256]{1,0:T(8,128)(2,1)S(1)} %copy-done.62, bf16[512,256]{1,0:T(8,128)(2,1)S(1)} %get-tuple-element.200.kr_a, ...), custom_call_target="tpu_custom_call" | custom-call | tf_op jit(solution)/shard_map/retain_back/pallas_call | solution.py:191
  258.7 4.6 %weight_parts.9 = (bf16[256,1024]{1,0:T(8,128)(2,1)S(1)}, bf16[512,1024]{1,0:T(8,128)(2,1)S(1)}, bf16[256,1024]{1,0:T(8,128)(2,1)S(1)}) custom-call(s32[8]{0:T(128)S(1)} %copy-done.85, bf16[512,2048]{1,0:T(8,128)(2,1)S(1)} %copy-done.6, bf16[512,2048]{1,0:T(8,128)(2,1)S(1)} %copy-done.8, bf16[512,512]{1,0:T(8,128)(2,1)S(1)} %get-tuple-element.285.refs_2_.dgate, ...), custom_call_target="tpu_custom_call" | custom-call | tf_op jit(solution)/shard_map/weight_parts/pallas_call | solution.py:641
  282.5 10.2 %collective-permute-done.49.refs_1_ = bf16[128,2048]{1,0:T(8,128)(2,1)S(1)} collective-permute-done((bf16[128,2048]{1,0:T(8,128)(2,1)S(1)}, bf16[128,2048]{1,0:T(8,128)(2,1)S(1)}, u32[]{:S(2)}, u32[]{:S(2)}) %collective-permute-start.49) | collective-permute-done | bytes 524320 | tf_op jit(solution)/shard_map/ppermute | solution.py:55
  302.3 7.8 %collective-permute-done.55.passed = bf16[128,2048]{1,0:T(8,128)(2,1)S(1)} collective-permute-done((bf16[128,2048]{1,0:T(8,128)(2,1)S(1)}, bf16[128,2048]{1,0:T(8,128)(2,1)S(1)}, u32[]{:S(2)}, u32[]{:S(2)}) %collective-permute-start.55) | collective-permute-done | bytes 524320 | tf_op jit(solution)/shard_map/ppermute | solution.py:69
  316.7 8.8 %collective-permute-done.58.up = bf16[128,2048]{1,0:T(8,128)(2,1)S(1)} collective-permute-done((bf16[128,2048]{1,0:T(8,128)(2,1)S(1)}, bf16[128,2048]{1,0:T(8,128)(2,1)S(1)}, u32[]{:S(2)}, u32[]{:S(2)}) %collective-permute-start.58) | collective-permute-done | bytes 524320 | tf_op jit(solution)/shard_map/ppermute | solution.py:55
  336.9 4.3 %collective-permute-done.64 = f32[5,2048]{1,0:T(8,128)S(1)} collective-permute-done((f32[5,2048]{1,0:T(8,128)S(1)}, f32[5,2048]{1,0:T(8,128)S(1)}, u32[]{:S(2)}, u32[]{:S(2)}) %collective-permute-start.64) | collective-permute-done | bytes 40992 | tf_op jit(solution)/shard_map/ppermute | solution.py:162
  356.4 5.3 %collective-permute-done.71.refs_3_ = bf16[256,1024]{1,0:T(8,128)(2,1)S(1)} collective-permute-done((bf16[256,1024]{1,0:T(8,128)(2,1)S(1)}, bf16[256,1024]{1,0:T(8,128)(2,1)S(1)}, u32[]{:S(2)}, u32[]{:S(2)}) %collective-permute-start.71) | collective-permute-done | bytes 524320 | tf_op jit(solution)/shard_map/ppermute | solution.py:69
  365.3 7.7 %collective-permute-done.74.both.refs_1_ = bf16[512,1024]{1,0:T(8,128)(2,1)S(1)} collective-permute-done((bf16[512,1024]{1,0:T(8,128)(2,1)S(1)}, bf16[512,1024]{1,0:T(8,128)(2,1)S(1)}, u32[]{:S(2)}, u32[]{:S(2)}) %collective-permute-start.74) | collective-permute-done | bytes 1048608 | tf_op jit(solution)/shard_map/ppermute | solution.py:69
  378.1 8.3 %placed.3 = (f32[2048,512]{1,0:T(8,128)}, f32[512,2048]{1,0:T(8,128)}) custom-call(s32[8]{0:T(128)S(1)} %stack.89.places, bf16[512,1024]{1,0:T(8,128)(2,1)} %copy-done.27, bf16[512,1024]{1,0:T(8,128)(2,1)} %copy-done.28, bf16[512,1024]{1,0:T(8,128)(2,1)} %copy-done.95, bf16[256,1024]{1,0:T(8,128)(2,1)} %copy-done.96, bf16[256,1024]{1,0:T(8,128)(2,1)} %copy-done.97), custom_call_target="tpu_custom_call" | custom-call | tf_op jit(solution)/shard_map/placed/pallas_call | solution.py:766
  393.4 6.4 %placed.4 = (f32[2048,512]{1,0:T(8,128)}, f32[512,2048]{1,0:T(8,128)}) custom-call(s32[8]{0:T(128)S(1)} %stack.89.places, bf16[512,1024]{1,0:T(8,128)(2,1)S(1)} %both.4.refs_0_, bf16[512,1024]{1,0:T(8,128)(2,1)S(1)} %copy-done.30, bf16[512,1024]{1,0:T(8,128)(2,1)S(1)} %collective-permute-done.81.refs_2_, bf16[256,1024]{1,0:T(8,128)(2,1)} %collective-permute-done.80.refs_3_, ...), custom_call_target="tpu_custom_call" | custom-call | tf_op jit(solution)/shard_map/placed/pallas_call | solution.py:766
  402.0 4.3 %collective-permute-done.86 = f32[6,2048]{1,0:T(8,128)S(1)} collective-permute-done((f32[6,2048]{1,0:T(8,128)S(1)}, f32[6,2048]{1,0:T(8,128)S(1)}, u32[]{:S(2)}, u32[]{:S(2)}) %collective-permute-start.86) | collective-permute-done | bytes 49184 | tf_op jit(solution)/shard_map/ppermute | solution.py:162
  413.4 5.1 %placed.5 = (f32[2048,256]{1,0:T(8,128)}, f32[2048,256]{1,0:T(8,128)}, f32[2048,512]{1,0:T(8,128)}) custom-call(s32[8]{0:T(128)S(1)} %stack.89.places, bf16[512,1024]{1,0:T(8,128)(2,1)S(1)} %both.5.refs_0_, bf16[512,1024]{1,0:T(8,128)(2,1)S(1)} %collective-permute-done.73.both.refs_1_, bf16[512,1024]{1,0:T(8,128)(2,1)S(1)} %collective-permute-done.87.refs_2_, ...), custom_call_target="tpu_custom_call" | custom-call | tf_op jit(solution)/shard_map/placed/pallas_call | solution.py:766
  (437 shorter events, 252.1 us)
Async XLA Ops:
  24.3 23.5 %collective-permute-start.5 = (bf16[128,2048]{1,0:T(8,128)(2,1)S(1)}, bf16[128,2048]{1,0:T(8,128)(2,1)}, u32[]{:S(2)}, u32[]{:S(2)}) collective-permute-start(bf16[128,2048]{1,0:T(8,128)(2,1)S(1)} %collective-permute-done.1.b3), channel_id=1, source_target_pairs={{1,0},{2,1},{3,2},{0,3},{5,4},{6,5},{7,6},{4,7},{9,8},{10,9},{11,1... | collective-permute-start | bytes 1572872 | tf_op jit(solution)/shard_map/ppermute | solution.py:55
  24.4 26.3 %collective-permute-start.6 = (bf16[128,2048]{1,0:T(8,128)(2,1)S(1)}, bf16[128,2048]{1,0:T(8,128)(2,1)}, u32[]{:S(2)}, u32[]{:S(2)}) collective-permute-start(bf16[128,2048]{1,0:T(8,128)(2,1)S(1)} %collective-permute-done.1.b3), channel_id=1, source_target_pairs={{3,0},{0,1},{1,2},{2,3},{7,4},{4,5},{5,6},{6,7},{11,8},{8,9},{9,10... | collective-permute-start | bytes 1572872 | tf_op jit(solution)/shard_map/ppermute | solution.py:55
  37.9 27.7 %collective-permute-start.8 = (bf16[128,2048]{1,0:T(8,128)(2,1)}, bf16[128,2048]{1,0:T(8,128)(2,1)S(1)}, u32[]{:S(2)}, u32[]{:S(2)}) collective-permute-start(bf16[128,2048]{1,0:T(8,128)(2,1)} %cot.1), channel_id=1, source_target_pairs={{1,0},{2,1},{3,2},{0,3},{5,4},{6,5},{7,6},{4,7},{9,8},{10,9},{11,1... | collective-permute-start | bytes 1572872 | tf_op jit(solution)/shard_map/ppermute | solution.py:55
  39.6 26.0 %collective-permute-start.9 = (bf16[128,2048]{1,0:T(8,128)(2,1)}, bf16[128,2048]{1,0:T(8,128)(2,1)S(1)}, u32[]{:S(2)}, u32[]{:S(2)}) collective-permute-start(bf16[128,2048]{1,0:T(8,128)(2,1)} %cot.1), channel_id=1, source_target_pairs={{3,0},{0,1},{1,2},{2,3},{7,4},{4,5},{5,6},{6,7},{11,8},{8,9},{9,10... | collective-permute-start | bytes 1572872 | tf_op jit(solution)/shard_map/ppermute | solution.py:55
  47.8 21.0 %collective-permute-start.10 = (bf16[128,2048]{1,0:T(8,128)(2,1)}, bf16[128,2048]{1,0:T(8,128)(2,1)S(1)}, u32[]{:S(2)}, u32[]{:S(2)}) collective-permute-start(bf16[128,2048]{1,0:T(8,128)(2,1)} %collective-permute-done.4.b3), channel_id=1, source_target_pairs={{1,0},{2,1},{3,2},{0,3},{5,4},{6,5},{7,6},{4,7},{9,8},{10,9},{11,1... | collective-permute-start | bytes 1572872 | tf_op jit(solution)/shard_map/ppermute | solution.py:55
  50.7 18.2 %collective-permute-start.11 = (bf16[128,2048]{1,0:T(8,128)(2,1)}, bf16[128,2048]{1,0:T(8,128)(2,1)S(1)}, u32[]{:S(2)}, u32[]{:S(2)}) collective-permute-start(bf16[128,2048]{1,0:T(8,128)(2,1)} %collective-permute-done.4.b3), channel_id=1, source_target_pairs={{3,0},{0,1},{1,2},{2,3},{7,4},{4,5},{5,6},{6,7},{11,8},{8,9},{9,10... | collective-permute-start | bytes 1572872 | tf_op jit(solution)/shard_map/ppermute | solution.py:55
  75.7 16.1 %collective-permute-start.15 = (bf16[128,2048]{1,0:T(8,128)(2,1)S(1)}, bf16[128,2048]{1,0:T(8,128)(2,1)S(1)}, u32[]{:S(2)}, u32[]{:S(2)}) collective-permute-start(bf16[128,2048]{1,0:T(8,128)(2,1)S(1)} %added.11), channel_id=1, source_target_pairs={{3,0},{0,1},{1,2},{2,3},{9,8},{10,9},{11,10},{8,11},{7,4},{4,5},{5... | collective-permute-start | bytes 1572872 | tf_op jit(solution)/shard_map/ppermute | solution.py:69
  78.0 22.4 %collective-permute-start.17 = (bf16[128,2048]{1,0:T(8,128)(2,1)S(1)}, bf16[128,2048]{1,0:T(8,128)(2,1)S(1)}, u32[]{:S(2)}, u32[]{:S(2)}) collective-permute-start(bf16[128,2048]{1,0:T(8,128)(2,1)S(1)} %added.12), channel_id=1, source_target_pairs={{4,0},{0,4},{5,1},{1,5},{6,2},{2,6},{7,3},{3,7},{12,8},{8,12},{13,... | collective-permute-start | bytes 1572872 | tf_op jit(solution)/shard_map/ppermute | solution.py:55
  80.2 19.0 %collective-permute-start.16 = (bf16[128,2048]{1,0:T(8,128)(2,1)S(1)}, bf16[128,2048]{1,0:T(8,128)(2,1)S(1)}, u32[]{:S(2)}, u32[]{:S(2)}) collective-permute-start(bf16[128,2048]{1,0:T(8,128)(2,1)S(1)} %chosen.5), channel_id=1, source_target_pairs={{1,0},{2,1},{3,2},{0,3},{11,8},{8,9},{9,10},{10,11},{5,4},{6,5},{7... | collective-permute-start | bytes 1572872 | tf_op jit(solution)/shard_map/ppermute | solution.py:69
  121.6 18.2 %collective-permute-start.25 = (bf16[128,2048]{1,0:T(8,128)(2,1)S(1)}, bf16[128,2048]{1,0:T(8,128)(2,1)S(1)}, u32[]{:S(2)}, u32[]{:S(2)}) collective-permute-start(bf16[128,2048]{1,0:T(8,128)(2,1)S(1)} %collective-permute-done.22.b3), channel_id=1, source_target_pairs={{1,0},{2,1},{3,2},{0,3},{5,4},{6,5},{7,6},{4,7},{9,8},{10,9},{11,1... | collective-permute-start | bytes 1572872 | tf_op jit(solution)/shard_map/ppermute | solution.py:55
  121.7 18.1 %collective-permute-start.26 = (bf16[128,2048]{1,0:T(8,128)(2,1)S(1)}, bf16[128,2048]{1,0:T(8,128)(2,1)S(1)}, u32[]{:S(2)}, u32[]{:S(2)}) collective-permute-start(bf16[128,2048]{1,0:T(8,128)(2,1)S(1)} %collective-permute-done.22.b3), channel_id=1, source_target_pairs={{3,0},{0,1},{1,2},{2,3},{7,4},{4,5},{5,6},{6,7},{11,8},{8,9},{9,10... | collective-permute-start | bytes 1572872 | tf_op jit(solution)/shard_map/ppermute | solution.py:55
  170.0 20.1 %collective-permute-start.33 = (bf16[128,2048]{1,0:T(8,128)(2,1)S(1)}, bf16[128,2048]{1,0:T(8,128)(2,1)S(1)}, u32[]{:S(2)}, u32[]{:S(2)}) collective-permute-start(bf16[128,2048]{1,0:T(8,128)(2,1)S(1)} %added.14), channel_id=1, source_target_pairs={{4,0},{0,4},{5,1},{1,5},{6,2},{2,6},{7,3},{3,7},{12,8},{8,12},{13,... | collective-permute-start | bytes 1572872 | tf_op jit(solution)/shard_map/ppermute | solution.py:55
  200.4 23.8 %collective-permute-start.41 = (bf16[512,1024]{1,0:T(8,128)(2,1)S(1)}, bf16[512,1024]{1,0:T(8,128)(2,1)S(1)}, u32[]{:S(2)}, u32[]{:S(2)}) collective-permute-start(bf16[512,1024]{1,0:T(8,128)(2,1)S(1)} %near.3), channel_id=1, source_target_pairs={{96,0},{0,32},{32,64},{64,96},{40,8},{72,40},{104,72},{8,104},{97,... | collective-permute-start | bytes 3145736 | tf_op jit(solution)/shard_map/ppermute | solution.py:69
  248.0 17.1 %collective-permute-start.47 = (bf16[256,1024]{1,0:T(8,128)(2,1)S(1)}, bf16[256,1024]{1,0:T(8,128)(2,1)S(1)}, u32[]{:S(2)}, u32[]{:S(2)}) collective-permute-start(bf16[256,1024]{1,0:T(8,128)(2,1)S(1)} %quarter.3.refs_0_), channel_id=1, source_target_pairs={{16,0},{0,16},{17,1},{1,17},{18,2},{2,18},{19,3},{3,19},{20,4},{4,... | collective-permute-start | bytes 1572872 | tf_op jit(solution)/shard_map/ppermute | solution.py:55
  278.0 17.2 %collective-permute-start.52 = (bf16[1024,1024]{1,0:T(8,128)(2,1)S(1)}, bf16[1024,1024]{1,0:T(8,128)(2,1)S(1)}, u32[]{:S(2)}, u32[]{:S(2)}) collective-permute-start(bf16[1024,1024]{1,0:T(8,128)(2,1)S(1)} %weight_parts.10), channel_id=1, source_target_pairs={{8,0},{0,8},{9,1},{1,9},{10,2},{2,10},{11,3},{3,11},{12,4},{4,12},... | collective-permute-start | bytes 6291464 | tf_op jit(solution)/shard_map/ppermute | solution.py:55
  278.1 21.3 %collective-permute-start.53 = (bf16[512,1024]{1,0:T(8,128)(2,1)S(1)}, bf16[512,1024]{1,0:T(8,128)(2,1)S(1)}, u32[]{:S(2)}, u32[]{:S(2)}) collective-permute-start(bf16[512,1024]{1,0:T(8,128)(2,1)S(1)} %near.4), channel_id=1, source_target_pairs={{96,0},{0,32},{32,64},{64,96},{40,8},{72,40},{104,72},{8,104},{97,... | collective-permute-start | bytes 3145736 | tf_op jit(solution)/shard_map/ppermute | solution.py:69
  299.6 16.4 %collective-permute-start.56 = (bf16[256,1024]{1,0:T(8,128)(2,1)S(1)}, bf16[256,1024]{1,0:T(8,128)(2,1)S(1)}, u32[]{:S(2)}, u32[]{:S(2)}) collective-permute-start(bf16[256,1024]{1,0:T(8,128)(2,1)S(1)} %get-tuple-element.318), channel_id=1, source_target_pairs={{96,0},{0,32},{32,64},{64,96},{40,8},{72,40},{104,72},{8,104},{97,... | collective-permute-start | bytes 1572872 | tf_op jit(solution)/shard_map/ppermute | solution.py:69
  300.6 16.1 %collective-permute-start.57 = (bf16[128,2048]{1,0:T(8,128)(2,1)S(1)}, bf16[128,2048]{1,0:T(8,128)(2,1)S(1)}, u32[]{:S(2)}, u32[]{:S(2)}) collective-permute-start(bf16[128,2048]{1,0:T(8,128)(2,1)S(1)} %added.17), channel_id=1, source_target_pairs={{4,0},{0,4},{5,1},{1,5},{6,2},{2,6},{7,3},{3,7},{12,8},{8,12},{13,... | collective-permute-start | bytes 1572872 | tf_op jit(solution)/shard_map/ppermute | solution.py:55
  316.2 16.5 %collective-permute-start.60 = (bf16[512,1024]{1,0:T(8,128)(2,1)S(1)}, bf16[512,1024]{1,0:T(8,128)(2,1)S(1)}, u32[]{:S(2)}, u32[]{:S(2)}) collective-permute-start(bf16[512,1024]{1,0:T(8,128)(2,1)S(1)} %near.5), channel_id=1, source_target_pairs={{96,0},{0,32},{32,64},{64,96},{40,8},{72,40},{104,72},{8,104},{97,... | collective-permute-start | bytes 3145736 | tf_op jit(solution)/shard_map/ppermute | solution.py:69
  332.7 16.0 %collective-permute-start.66 = (bf16[512,1024]{1,0:T(8,128)(2,1)S(1)}, bf16[512,1024]{1,0:T(8,128)(2,1)S(1)}, u32[]{:S(2)}, u32[]{:S(2)}) collective-permute-start(bf16[512,1024]{1,0:T(8,128)(2,1)S(1)} %both.3.refs_0_), channel_id=1, source_target_pairs={{96,0},{0,32},{32,64},{64,96},{40,8},{72,40},{104,72},{8,104},{97,... | collective-permute-start | bytes 3145736 | tf_op jit(solution)/shard_map/ppermute | solution.py:69
  332.7 16.1 %collective-permute-start.67 = (bf16[256,1024]{1,0:T(8,128)(2,1)S(1)}, bf16[256,1024]{1,0:T(8,128)(2,1)S(1)}, u32[]{:S(2)}, u32[]{:S(2)}) collective-permute-start(bf16[256,1024]{1,0:T(8,128)(2,1)S(1)} %added.15.first), channel_id=1, source_target_pairs={{8,0},{0,8},{9,1},{1,9},{10,2},{2,10},{11,3},{3,11},{12,4},{4,12},... | collective-permute-start | bytes 1572872 | tf_op jit(solution)/shard_map/ppermute | solution.py:55
  351.5 21.5 %collective-permute-start.74 = (bf16[512,1024]{1,0:T(8,128)(2,1)S(1)}, bf16[512,1024]{1,0:T(8,128)(2,1)S(1)}, u32[]{:S(2)}, u32[]{:S(2)}) collective-permute-start(bf16[512,1024]{1,0:T(8,128)(2,1)S(1)} %both.4.refs_0_), channel_id=1, source_target_pairs={{96,0},{0,32},{32,64},{64,96},{40,8},{72,40},{104,72},{8,104},{97,... | collective-permute-start | bytes 3145736 | tf_op jit(solution)/shard_map/ppermute | solution.py:69
  361.8 24.7 %collective-permute-start.73 = (bf16[512,1024]{1,0:T(8,128)(2,1)S(1)}, bf16[512,1024]{1,0:T(8,128)(2,1)S(1)}, u32[]{:S(2)}, u32[]{:S(2)}) collective-permute-start(bf16[512,1024]{1,0:T(8,128)(2,1)S(1)} %both.5.refs_0_), channel_id=1, source_target_pairs={{96,0},{0,32},{32,64},{64,96},{40,8},{72,40},{104,72},{8,104},{97,... | collective-permute-start | bytes 3145736 | tf_op jit(solution)/shard_map/ppermute | solution.py:69
  365.3 21.3 %collective-permute-start.77 = (bf16[128,2048]{1,0:T(8,128)(2,1)}, bf16[128,2048]{1,0:T(8,128)(2,1)}, u32[]{:S(2)}, u32[]{:S(2)}) collective-permute-start(bf16[128,2048]{1,0:T(8,128)(2,1)} %get-tuple-element.345), channel_id=1, source_target_pairs={{4,0},{0,4},{5,1},{1,5},{6,2},{2,6},{7,3},{3,7},{12,8},{8,12},{13,... | collective-permute-start | bytes 1572872 | tf_op jit(solution)/shard_map/ppermute | solution.py:55
  (168 other events, 1679.0 us)

commit v3 on v2

--- a/solution.py
+++ b/solution.py
@@ -949,10 +949,10 @@
     out_rs = Scatter({**out_a, **{p: line.hold(v) for p, v in out_b.items()}})
     gate_sums.swap(line)
     sums.step(line)
-    feed_sums.last(line)
     gate_pieces = [in_hbm(p) for p in gate_sums.pieces(line)]
     grad_gate, grad_out = placed(gate_pieces, final, (DV, DV), (False, True))
     line.done(grad_gate)
+    feed_sums.last(line)
     head_sums.last(line)
     out_rs.relay(line)
     out_rs.side(line)

time: 432 us -> 438 us (1.014)
  waiting for transfers between devices: 185 us -> 191 us
    ppermute x20, waiting for transfers between devices: 72.5 us -> 78.4 us  [by_sides(): return lax.ppermute(value, names, pairs)]
    unnamed x198 -> x192, local copies, waits for them, and re-layouts: 26.6 us -> 28.1 us
  transfers between devices with their start and end apart: 93 -> 93, of which waited for: 49 -> 51; matrix products, arithmetic and copies ran while one was open for 1% -> 1% of each run, Pallas kernels for 22% -> 21%
where the time goes in v3:
time: 438 us; the launch traced here: 432 us
  waiting for transfers between devices  191 us (44%)
  Pallas kernels  112 us (26%)
  starting transfers between devices  92.5 us (21%)
  local copies, waits for them, and re-layouts  31.9 us (7%)
    ppermute x66, waiting for transfers between devices, shifted(): lax.ppermute(value, axis, [((i + step) % size, i) for i in range(size)])  94.3 us
    ppermute x20, waiting for transfers between devices, by_sides(): return lax.ppermute(value, names, pairs)  78.4 us
    ppermute x66, starting transfers between devices, shifted(): lax.ppermute(value, axis, [((i + step) % size, i) for i in range(size)])  76.5 us
    pallas_call x50, Pallas kernels, simple(): pl.pallas_call(body, in_specs=in_specs, out_specs=[pl.BlockSpec(memory_sp...  65.9 us
    unnamed x192, local copies, waits for them, and re-layouts  28.1 us
    pallas_call x6, Pallas kernels, weight_parts(): pl.pallas_call(functools.partial(weight_kernel, counts=[len(lefts) for le...  25.6 us
    pallas_call x3, Pallas kernels, placed(): pl.pallas_call(functools.partial(place_kernel, columns=columns, turned=tu...  20.5 us
    ppermute x7, waiting for transfers between devices, step(): self.come = lax.ppermute(self.value, axis, pairs)  18.1 us
  transfers between devices with their start and end apart: 93, of which 51 were waited for; matrix products, arithmetic and copies ran while one was open for 1% of the time, Pallas kernels for 21%

profile of v3, /device:TPU:0, one launch (start us, length us, event | category | flops | bytes accessed | tf_op | source)
XLA Modules:
  0.0 431.6 jit_solution(12155790873525026528)
XLA Ops:
  12.1 6.8 %collective-permute-done.first.b1 = bf16[128,2048]{1,0:T(8,128)(2,1)S(1)} collective-permute-done((bf16[128,2048]{1,0:T(8,128)(2,1)S(1)}, bf16[128,2048]{1,0:T(8,128)(2,1)S(1)}, u32[]{:S(2)}, u32[]{:S(2)}) %collective-permute-start) | collective-permute-done | bytes 524320 | tf_op jit(solution)/shard_map/ppermute | solution.py:55
  26.3 9.9 %collective-permute-done.3.b0 = bf16[128,2048]{1,0:T(8,128)(2,1)} collective-permute-done((bf16[128,2048]{1,0:T(8,128)(2,1)S(1)}, bf16[128,2048]{1,0:T(8,128)(2,1)}, u32[]{:S(2)}, u32[]{:S(2)}) %collective-permute-start.3) | collective-permute-done | bytes 524320 | tf_op jit(solution)/shard_map/ppermute | solution.py:69
  40.0 6.4 %heads.2 = (bf16[512,2048]{1,0:T(8,128)(2,1)S(1)}, bf16[512,256]{1,0:T(8,128)(2,1)S(1)}, bf16[512,256]{1,0:T(8,128)(2,1)S(1)}, bf16[512,512]{1,0:T(8,128)(2,1)S(1)}, f32[512,512]{1,0:T(8,128)S(1)}) custom-call(s32[10]{0:T(128)S(1)} %stack.77.marks, bf16[128,2048]{1,0:T(8,128)(2,1)S(1)} %norm.1.b0, bf16[128,2048]{1,0:T(8,128)(2,1)S(1)} %collective-permute-done.first.b1, ...), custom_call_target="tpu_custom_call" | custom-call | tf_op jit(solution)/shard_map/heads/pallas_call | solution.py:191
  50.8 7.1 %heads.3 = (bf16[512,2048]{1,0:T(8,128)(2,1)S(1)}, bf16[512,256]{1,0:T(8,128)(2,1)S(1)}, bf16[512,256]{1,0:T(8,128)(2,1)S(1)}, bf16[512,512]{1,0:T(8,128)(2,1)S(1)}, f32[512,512]{1,0:T(8,128)S(1)}) custom-call(s32[10]{0:T(128)S(1)} %stack.77.marks, bf16[128,2048]{1,0:T(8,128)(2,1)} %collective-permute-done.3.b0, ...), custom_call_target="tpu_custom_call" | custom-call | tf_op jit(solution)/shard_map/heads/pallas_call | solution.py:191
  83.8 7.8 %collective-permute-done.15.passed = bf16[128,2048]{1,0:T(8,128)(2,1)S(1)} collective-permute-done((bf16[128,2048]{1,0:T(8,128)(2,1)S(1)}, bf16[128,2048]{1,0:T(8,128)(2,1)S(1)}, u32[]{:S(2)}, u32[]{:S(2)}) %collective-permute-start.15) | collective-permute-done | bytes 524320 | tf_op jit(solution)/shard_map/ppermute | solution.py:69
  123.5 7.1 %collective-permute-done.24.b0 = bf16[128,2048]{1,0:T(8,128)(2,1)S(1)} collective-permute-done((bf16[128,2048]{1,0:T(8,128)(2,1)S(1)}, bf16[128,2048]{1,0:T(8,128)(2,1)S(1)}, u32[]{:S(2)}, u32[]{:S(2)}) %collective-permute-start.24) | collective-permute-done | bytes 524320 | tf_op jit(solution)/shard_map/ppermute | solution.py:69
  171.4 10.2 %collective-permute-done.31.passed = bf16[128,2048]{1,0:T(8,128)(2,1)S(1)} collective-permute-done((bf16[128,2048]{1,0:T(8,128)(2,1)S(1)}, bf16[128,2048]{1,0:T(8,128)(2,1)S(1)}, u32[]{:S(2)}, u32[]{:S(2)}) %collective-permute-start.31) | collective-permute-done | bytes 524320 | tf_op jit(solution)/shard_map/ppermute | solution.py:69
  185.2 4.6 %weight_parts.7 = (bf16[256,1024]{1,0:T(8,128)(2,1)S(1)}, bf16[512,1024]{1,0:T(8,128)(2,1)S(1)}, bf16[256,1024]{1,0:T(8,128)(2,1)S(1)}) custom-call(s32[8]{0:T(128)S(1)} %copy-done.82, bf16[512,2048]{1,0:T(8,128)(2,1)S(1)} %copy-done.17, bf16[512,2048]{1,0:T(8,128)(2,1)S(1)} %copy-done.19, bf16[512,512]{1,0:T(8,128)(2,1)S(1)} %copy-done.42, ...), custom_call_target="tpu_custom_call" | custom-call | tf_op jit(solution)/shard_map/weight_parts/pallas_call | solution.py:641
  202.9 7.1 %collective-permute-done.36.first.b1 = bf16[128,2048]{1,0:T(8,128)(2,1)S(1)} collective-permute-done((bf16[128,2048]{1,0:T(8,128)(2,1)S(1)}, bf16[128,2048]{1,0:T(8,128)(2,1)S(1)}, u32[]{:S(2)}, u32[]{:S(2)}) %collective-permute-start.36) | collective-permute-done | bytes 524320 | tf_op jit(solution)/shard_map/ppermute | solution.py:55
  213.8 8.9 %collective-permute-done.40.b0 = bf16[128,2048]{1,0:T(8,128)(2,1)S(1)} collective-permute-done((bf16[128,2048]{1,0:T(8,128)(2,1)S(1)}, bf16[128,2048]{1,0:T(8,128)(2,1)S(1)}, u32[]{:S(2)}, u32[]{:S(2)}) %collective-permute-start.40) | collective-permute-done | bytes 524320 | tf_op jit(solution)/shard_map/ppermute | solution.py:69
  228.9 10.3 %collective-permute-done.43.b1 = bf16[128,2048]{1,0:T(8,128)(2,1)S(1)} collective-permute-done((bf16[128,2048]{1,0:T(8,128)(2,1)S(1)}, bf16[128,2048]{1,0:T(8,128)(2,1)S(1)}, u32[]{:S(2)}, u32[]{:S(2)}) %collective-permute-start.43) | collective-permute-done | bytes 524320 | tf_op jit(solution)/shard_map/ppermute | solution.py:55
  251.8 7.3 %retain_back.1 = (bf16[512,1024]{1,0:T(8,128)(2,1)S(1)}, bf16[512,1024]{1,0:T(8,128)(2,1)S(1)}) custom-call(s32[10]{0:T(128)S(1)} %copy-done.84, f32[1]{0:T(128)} %bitcast.11.decay, bf16[512,256]{1,0:T(8,128)(2,1)S(1)} %copy-done.57, bf16[512,256]{1,0:T(8,128)(2,1)S(1)} %copy-done.59, bf16[512,256]{1,0:T(8,128)(2,1)S(1)} %get-tuple-element.200.kr_a, ...), custom_call_target="tpu_custom_call" | custom-call | tf_op jit(solution)/shard_map/retain_back/pallas_call | solution.py:191
  259.1 4.6 %weight_parts.9 = (bf16[256,1024]{1,0:T(8,128)(2,1)S(1)}, bf16[512,1024]{1,0:T(8,128)(2,1)S(1)}, bf16[256,1024]{1,0:T(8,128)(2,1)S(1)}) custom-call(s32[8]{0:T(128)S(1)} %copy-done.82, bf16[512,2048]{1,0:T(8,128)(2,1)S(1)} %copy-done.6, bf16[512,2048]{1,0:T(8,128)(2,1)S(1)} %copy-done.8, bf16[512,512]{1,0:T(8,128)(2,1)S(1)} %get-tuple-element.285.refs_2_.dgate, ...), custom_call_target="tpu_custom_call" | custom-call | tf_op jit(solution)/shard_map/weight_parts/pallas_call | solution.py:641
  283.3 9.9 %collective-permute-done.49.refs_1_ = bf16[128,2048]{1,0:T(8,128)(2,1)S(1)} collective-permute-done((bf16[128,2048]{1,0:T(8,128)(2,1)S(1)}, bf16[128,2048]{1,0:T(8,128)(2,1)S(1)}, u32[]{:S(2)}, u32[]{:S(2)}) %collective-permute-start.49) | collective-permute-done | bytes 524320 | tf_op jit(solution)/shard_map/ppermute | solution.py:55
  303.1 7.8 %collective-permute-done.55.passed = bf16[128,2048]{1,0:T(8,128)(2,1)S(1)} collective-permute-done((bf16[128,2048]{1,0:T(8,128)(2,1)S(1)}, bf16[128,2048]{1,0:T(8,128)(2,1)S(1)}, u32[]{:S(2)}, u32[]{:S(2)}) %collective-permute-start.55) | collective-permute-done | bytes 524320 | tf_op jit(solution)/shard_map/ppermute | solution.py:69
  317.2 9.0 %collective-permute-done.58.up = bf16[128,2048]{1,0:T(8,128)(2,1)S(1)} collective-permute-done((bf16[128,2048]{1,0:T(8,128)(2,1)S(1)}, bf16[128,2048]{1,0:T(8,128)(2,1)S(1)}, u32[]{:S(2)}, u32[]{:S(2)}) %collective-permute-start.58) | collective-permute-done | bytes 524320 | tf_op jit(solution)/shard_map/ppermute | solution.py:55
  337.6 4.3 collective-permute-done.64
  343.0 4.4 %collective-permute-done.65 = f32[5,2048]{1,0:T(8,128)S(1)} collective-permute-done((f32[5,2048]{1,0:T(8,128)S(1)}, f32[5,2048]{1,0:T(8,128)S(1)}, u32[]{:S(2)}, u32[]{:S(2)}) %collective-permute-start.65) | collective-permute-done | bytes 40992 | tf_op jit(solution)/shard_map/ppermute | solution.py:162
  356.9 5.4 %collective-permute-done.71.refs_3_ = bf16[256,1024]{1,0:T(8,128)(2,1)} collective-permute-done((bf16[256,1024]{1,0:T(8,128)(2,1)S(1)}, bf16[256,1024]{1,0:T(8,128)(2,1)}, u32[]{:S(2)}, u32[]{:S(2)}) %collective-permute-start.71) | collective-permute-done | bytes 524320 | tf_op jit(solution)/shard_map/ppermute | solution.py:69
  369.4 8.3 %placed.3 = (f32[2048,512]{1,0:T(8,128)}, f32[512,2048]{1,0:T(8,128)}) custom-call(s32[8]{0:T(128)S(1)} %stack.89.places, bf16[512,1024]{1,0:T(8,128)(2,1)} %copy-done.27, bf16[512,1024]{1,0:T(8,128)(2,1)} %collective-permute-done.66.both.refs_1_, bf16[512,1024]{1,0:T(8,128)(2,1)} %collective-permute-done.75.refs_2_, ...), custom_call_target="tpu_custom_call" | custom-call | tf_op jit(solution)/shard_map/placed/pallas_call | solution.py:766
  379.9 9.7 %collective-permute-done.73.both.refs_1_ = bf16[512,1024]{1,0:T(8,128)(2,1)S(1)} collective-permute-done((bf16[512,1024]{1,0:T(8,128)(2,1)S(1)}, bf16[512,1024]{1,0:T(8,128)(2,1)S(1)}, u32[]{:S(2)}, u32[]{:S(2)}) %collective-permute-start.73) | collective-permute-done | bytes 1048608 | tf_op jit(solution)/shard_map/ppermute | solution.py:69
  390.0 5.2 %collective-permute-done.80.refs_3_ = bf16[256,1024]{1,0:T(8,128)(2,1)S(1)} collective-permute-done((bf16[256,1024]{1,0:T(8,128)(2,1)S(1)}, bf16[256,1024]{1,0:T(8,128)(2,1)S(1)}, u32[]{:S(2)}, u32[]{:S(2)}) %collective-permute-start.80) | collective-permute-done | bytes 524320 | tf_op jit(solution)/shard_map/ppermute | solution.py:69
  398.8 7.1 %placed.4 = (f32[2048,512]{1,0:T(8,128)}, f32[512,2048]{1,0:T(8,128)}) custom-call(s32[8]{0:T(128)S(1)} %stack.89.places, bf16[512,1024]{1,0:T(8,128)(2,1)S(1)} %both.4.refs_0_, bf16[512,1024]{1,0:T(8,128)(2,1)} %collective-permute-done.74.both.refs_1_, bf16[512,1024]{1,0:T(8,128)(2,1)S(1)} %collective-permute-done.81.refs_2_, ...), custom_call_target="tpu_custom_call" | custom-call | tf_op jit(solution)/shard_map/placed/pallas_call | solution.py:766
  417.8 5.1 %placed.5 = (f32[2048,256]{1,0:T(8,128)}, f32[2048,256]{1,0:T(8,128)}, f32[2048,512]{1,0:T(8,128)}) custom-call(s32[8]{0:T(128)S(1)} %stack.89.places, bf16[512,1024]{1,0:T(8,128)(2,1)S(1)} %both.5.refs_0_, bf16[512,1024]{1,0:T(8,128)(2,1)S(1)} %collective-permute-done.73.both.refs_1_, bf16[512,1024]{1,0:T(8,128)(2,1)S(1)} %collective-permute-done.87.refs_2_, ...), custom_call_target="tpu_custom_call" | custom-call | tf_op jit(solution)/shard_map/placed/pallas_call | solution.py:766
  (431 shorter events, 254.9 us)
Async XLA Ops:
  24.3 23.5 %collective-permute-start.5 = (bf16[128,2048]{1,0:T(8,128)(2,1)S(1)}, bf16[128,2048]{1,0:T(8,128)(2,1)}, u32[]{:S(2)}, u32[]{:S(2)}) collective-permute-start(bf16[128,2048]{1,0:T(8,128)(2,1)S(1)} %collective-permute-done.1.b3), channel_id=1, source_target_pairs={{1,0},{2,1},{3,2},{0,3},{5,4},{6,5},{7,6},{4,7},{9,8},{10,9},{11,1... | collective-permute-start | bytes 1572872 | tf_op jit(solution)/shard_map/ppermute | solution.py:55
  24.4 26.3 %collective-permute-start.6 = (bf16[128,2048]{1,0:T(8,128)(2,1)S(1)}, bf16[128,2048]{1,0:T(8,128)(2,1)}, u32[]{:S(2)}, u32[]{:S(2)}) collective-permute-start(bf16[128,2048]{1,0:T(8,128)(2,1)S(1)} %collective-permute-done.1.b3), channel_id=1, source_target_pairs={{3,0},{0,1},{1,2},{2,3},{7,4},{4,5},{5,6},{6,7},{11,8},{8,9},{9,10... | collective-permute-start | bytes 1572872 | tf_op jit(solution)/shard_map/ppermute | solution.py:55
  37.9 27.5 %collective-permute-start.8 = (bf16[128,2048]{1,0:T(8,128)(2,1)}, bf16[128,2048]{1,0:T(8,128)(2,1)S(1)}, u32[]{:S(2)}, u32[]{:S(2)}) collective-permute-start(bf16[128,2048]{1,0:T(8,128)(2,1)} %cot.1), channel_id=1, source_target_pairs={{1,0},{2,1},{3,2},{0,3},{5,4},{6,5},{7,6},{4,7},{9,8},{10,9},{11,1... | collective-permute-start | bytes 1572872 | tf_op jit(solution)/shard_map/ppermute | solution.py:55
  39.6 25.8 %collective-permute-start.9 = (bf16[128,2048]{1,0:T(8,128)(2,1)}, bf16[128,2048]{1,0:T(8,128)(2,1)S(1)}, u32[]{:S(2)}, u32[]{:S(2)}) collective-permute-start(bf16[128,2048]{1,0:T(8,128)(2,1)} %cot.1), channel_id=1, source_target_pairs={{3,0},{0,1},{1,2},{2,3},{7,4},{4,5},{5,6},{6,7},{11,8},{8,9},{9,10... | collective-permute-start | bytes 1572872 | tf_op jit(solution)/shard_map/ppermute | solution.py:55
  47.8 20.9 %collective-permute-start.10 = (bf16[128,2048]{1,0:T(8,128)(2,1)}, bf16[128,2048]{1,0:T(8,128)(2,1)S(1)}, u32[]{:S(2)}, u32[]{:S(2)}) collective-permute-start(bf16[128,2048]{1,0:T(8,128)(2,1)} %collective-permute-done.4.b3), channel_id=1, source_target_pairs={{1,0},{2,1},{3,2},{0,3},{5,4},{6,5},{7,6},{4,7},{9,8},{10,9},{11,1... | collective-permute-start | bytes 1572872 | tf_op jit(solution)/shard_map/ppermute | solution.py:55
  50.6 18.1 %collective-permute-start.11 = (bf16[128,2048]{1,0:T(8,128)(2,1)}, bf16[128,2048]{1,0:T(8,128)(2,1)S(1)}, u32[]{:S(2)}, u32[]{:S(2)}) collective-permute-start(bf16[128,2048]{1,0:T(8,128)(2,1)} %collective-permute-done.4.b3), channel_id=1, source_target_pairs={{3,0},{0,1},{1,2},{2,3},{7,4},{4,5},{5,6},{6,7},{11,8},{8,9},{9,10... | collective-permute-start | bytes 1572872 | tf_op jit(solution)/shard_map/ppermute | solution.py:55
  77.8 22.4 %collective-permute-start.17 = (bf16[128,2048]{1,0:T(8,128)(2,1)S(1)}, bf16[128,2048]{1,0:T(8,128)(2,1)S(1)}, u32[]{:S(2)}, u32[]{:S(2)}) collective-permute-start(bf16[128,2048]{1,0:T(8,128)(2,1)S(1)} %added.12), channel_id=1, source_target_pairs={{4,0},{0,4},{5,1},{1,5},{6,2},{2,6},{7,3},{3,7},{12,8},{8,12},{13,... | collective-permute-start | bytes 1572872 | tf_op jit(solution)/shard_map/ppermute | solution.py:55
  80.0 19.0 %collective-permute-start.16 = (bf16[128,2048]{1,0:T(8,128)(2,1)S(1)}, bf16[128,2048]{1,0:T(8,128)(2,1)S(1)}, u32[]{:S(2)}, u32[]{:S(2)}) collective-permute-start(bf16[128,2048]{1,0:T(8,128)(2,1)S(1)} %chosen.5), channel_id=1, source_target_pairs={{1,0},{2,1},{3,2},{0,3},{11,8},{8,9},{9,10},{10,11},{5,4},{6,5},{7... | collective-permute-start | bytes 1572872 | tf_op jit(solution)/shard_map/ppermute | solution.py:69
  121.4 18.2 %collective-permute-start.25 = (bf16[128,2048]{1,0:T(8,128)(2,1)S(1)}, bf16[128,2048]{1,0:T(8,128)(2,1)S(1)}, u32[]{:S(2)}, u32[]{:S(2)}) collective-permute-start(bf16[128,2048]{1,0:T(8,128)(2,1)S(1)} %collective-permute-done.22.b3), channel_id=1, source_target_pairs={{1,0},{2,1},{3,2},{0,3},{5,4},{6,5},{7,6},{4,7},{9,8},{10,9},{11,1... | collective-permute-start | bytes 1572872 | tf_op jit(solution)/shard_map/ppermute | solution.py:55
  121.5 18.1 %collective-permute-start.26 = (bf16[128,2048]{1,0:T(8,128)(2,1)S(1)}, bf16[128,2048]{1,0:T(8,128)(2,1)S(1)}, u32[]{:S(2)}, u32[]{:S(2)}) collective-permute-start(bf16[128,2048]{1,0:T(8,128)(2,1)S(1)} %collective-permute-done.22.b3), channel_id=1, source_target_pairs={{3,0},{0,1},{1,2},{2,3},{7,4},{4,5},{5,6},{6,7},{11,8},{8,9},{9,10... | collective-permute-start | bytes 1572872 | tf_op jit(solution)/shard_map/ppermute | solution.py:55
  171.2 20.3 %collective-permute-start.33 = (bf16[128,2048]{1,0:T(8,128)(2,1)S(1)}, bf16[128,2048]{1,0:T(8,128)(2,1)S(1)}, u32[]{:S(2)}, u32[]{:S(2)}) collective-permute-start(bf16[128,2048]{1,0:T(8,128)(2,1)S(1)} %added.14), channel_id=1, source_target_pairs={{4,0},{0,4},{5,1},{1,5},{6,2},{2,6},{7,3},{3,7},{12,8},{8,12},{13,... | collective-permute-start | bytes 1572872 | tf_op jit(solution)/shard_map/ppermute | solution.py:55
  201.2 23.4 %collective-permute-start.41 = (bf16[512,1024]{1,0:T(8,128)(2,1)S(1)}, bf16[512,1024]{1,0:T(8,128)(2,1)S(1)}, u32[]{:S(2)}, u32[]{:S(2)}) collective-permute-start(bf16[512,1024]{1,0:T(8,128)(2,1)S(1)} %near.3), channel_id=1, source_target_pairs={{96,0},{0,32},{32,64},{64,96},{40,8},{72,40},{104,72},{8,104},{97,... | collective-permute-start | bytes 3145736 | tf_op jit(solution)/shard_map/ppermute | solution.py:69
  248.5 16.9 %collective-permute-start.47 = (bf16[256,1024]{1,0:T(8,128)(2,1)S(1)}, bf16[256,1024]{1,0:T(8,128)(2,1)S(1)}, u32[]{:S(2)}, u32[]{:S(2)}) collective-permute-start(bf16[256,1024]{1,0:T(8,128)(2,1)S(1)} %quarter.3.refs_0_), channel_id=1, source_target_pairs={{16,0},{0,16},{17,1},{1,17},{18,2},{2,18},{19,3},{3,19},{20,4},{4,... | collective-permute-start | bytes 1572872 | tf_op jit(solution)/shard_map/ppermute | solution.py:55
  278.4 17.6 %collective-permute-start.52 = (bf16[1024,1024]{1,0:T(8,128)(2,1)S(1)}, bf16[1024,1024]{1,0:T(8,128)(2,1)S(1)}, u32[]{:S(2)}, u32[]{:S(2)}) collective-permute-start(bf16[1024,1024]{1,0:T(8,128)(2,1)S(1)} %weight_parts.10), channel_id=1, source_target_pairs={{8,0},{0,8},{9,1},{1,9},{10,2},{2,10},{11,3},{3,11},{12,4},{4,12},... | collective-permute-start | bytes 6291464 | tf_op jit(solution)/shard_map/ppermute | solution.py:55
  278.5 21.7 %collective-permute-start.53 = (bf16[512,1024]{1,0:T(8,128)(2,1)S(1)}, bf16[512,1024]{1,0:T(8,128)(2,1)S(1)}, u32[]{:S(2)}, u32[]{:S(2)}) collective-permute-start(bf16[512,1024]{1,0:T(8,128)(2,1)S(1)} %near.4), channel_id=1, source_target_pairs={{96,0},{0,32},{32,64},{64,96},{40,8},{72,40},{104,72},{8,104},{97,... | collective-permute-start | bytes 3145736 | tf_op jit(solution)/shard_map/ppermute | solution.py:69
  300.4 16.2 %collective-permute-start.56 = (bf16[256,1024]{1,0:T(8,128)(2,1)S(1)}, bf16[256,1024]{1,0:T(8,128)(2,1)S(1)}, u32[]{:S(2)}, u32[]{:S(2)}) collective-permute-start(bf16[256,1024]{1,0:T(8,128)(2,1)S(1)} %get-tuple-element.318), channel_id=1, source_target_pairs={{96,0},{0,32},{32,64},{64,96},{40,8},{72,40},{104,72},{8,104},{97,... | collective-permute-start | bytes 1572872 | tf_op jit(solution)/shard_map/ppermute | solution.py:69
  316.7 16.5 %collective-permute-start.60 = (bf16[512,1024]{1,0:T(8,128)(2,1)S(1)}, bf16[512,1024]{1,0:T(8,128)(2,1)S(1)}, u32[]{:S(2)}, u32[]{:S(2)}) collective-permute-start(bf16[512,1024]{1,0:T(8,128)(2,1)S(1)} %near.5), channel_id=1, source_target_pairs={{96,0},{0,32},{32,64},{64,96},{40,8},{72,40},{104,72},{8,104},{97,... | collective-permute-start | bytes 3145736 | tf_op jit(solution)/shard_map/ppermute | solution.py:69
  333.2 16.1 %collective-permute-start.66 = (bf16[512,1024]{1,0:T(8,128)(2,1)S(1)}, bf16[512,1024]{1,0:T(8,128)(2,1)}, u32[]{:S(2)}, u32[]{:S(2)}) collective-permute-start(bf16[512,1024]{1,0:T(8,128)(2,1)S(1)} %both.3.refs_0_), channel_id=1, source_target_pairs={{96,0},{0,32},{32,64},{64,96},{40,8},{72,40},{104,72},{8,104},{97,... | collective-permute-start | bytes 3145736 | tf_op jit(solution)/shard_map/ppermute | solution.py:69
  333.2 17.4 %collective-permute-start.67 = (bf16[256,1024]{1,0:T(8,128)(2,1)S(1)}, bf16[256,1024]{1,0:T(8,128)(2,1)S(1)}, u32[]{:S(2)}, u32[]{:S(2)}) collective-permute-start(bf16[256,1024]{1,0:T(8,128)(2,1)S(1)} %added.15.first), channel_id=1, source_target_pairs={{8,0},{0,8},{9,1},{1,9},{10,2},{2,10},{11,3},{3,11},{12,4},{4,12},... | collective-permute-start | bytes 1572872 | tf_op jit(solution)/shard_map/ppermute | solution.py:55
  362.3 16.1 %collective-permute-start.74 = (bf16[512,1024]{1,0:T(8,128)(2,1)S(1)}, bf16[512,1024]{1,0:T(8,128)(2,1)}, u32[]{:S(2)}, u32[]{:S(2)}) collective-permute-start(bf16[512,1024]{1,0:T(8,128)(2,1)S(1)} %both.4.refs_0_), channel_id=1, source_target_pairs={{96,0},{0,32},{32,64},{64,96},{40,8},{72,40},{104,72},{8,104},{97,... | collective-permute-start | bytes 3145736 | tf_op jit(solution)/shard_map/ppermute | solution.py:69
  362.4 27.2 %collective-permute-start.73 = (bf16[512,1024]{1,0:T(8,128)(2,1)S(1)}, bf16[512,1024]{1,0:T(8,128)(2,1)S(1)}, u32[]{:S(2)}, u32[]{:S(2)}) collective-permute-start(bf16[512,1024]{1,0:T(8,128)(2,1)S(1)} %both.5.refs_0_), channel_id=1, source_target_pairs={{96,0},{0,32},{32,64},{64,96},{40,8},{72,40},{104,72},{8,104},{97,... | collective-permute-start | bytes 3145736 | tf_op jit(solution)/shard_map/ppermute | solution.py:69
  365.2 24.4 %collective-permute-start.77 = (bf16[128,2048]{1,0:T(8,128)(2,1)}, bf16[128,2048]{1,0:T(8,128)(2,1)S(1)}, u32[]{:S(2)}, u32[]{:S(2)}) collective-permute-start(bf16[128,2048]{1,0:T(8,128)(2,1)} %copy-done.94), channel_id=1, source_target_pairs={{4,0},{0,4},{5,1},{1,5},{6,2},{2,6},{7,3},{3,7},{12,8},{8,12},{13,... | collective-permute-start | bytes 1572872 | tf_op jit(solution)/shard_map/ppermute | solution.py:55
  366.2 23.6 %collective-permute-start.78 = (bf16[128,2048]{1,0:T(8,128)(2,1)}, bf16[128,2048]{1,0:T(8,128)(2,1)S(1)}, u32[]{:S(2)}, u32[]{:S(2)}) collective-permute-start(bf16[128,2048]{1,0:T(8,128)(2,1)} %copy-done.93), channel_id=1, source_target_pairs={{3,0},{0,1},{1,2},{2,3},{7,4},{4,5},{5,6},{6,7},{11,8},{8,9},{9,10... | collective-permute-start | bytes 1572872 | tf_op jit(solution)/shard_map/ppermute | solution.py:55
  366.2 23.6 %collective-permute-start.79 = (bf16[128,2048]{1,0:T(8,128)(2,1)}, bf16[128,2048]{1,0:T(8,128)(2,1)S(1)}, u32[]{:S(2)}, u32[]{:S(2)}) collective-permute-start(bf16[128,2048]{1,0:T(8,128)(2,1)} %copy-done.92), channel_id=1, source_target_pairs={{1,0},{2,1},{3,2},{0,3},{5,4},{6,5},{7,6},{4,7},{9,8},{10,9},{11,1... | collective-permute-start | bytes 1572872 | tf_op jit(solution)/shard_map/ppermute | solution.py:55
  (165 other events, 1654.2 us)
